TPU v7x, 32 devices: a whole 2x2x4 slice. The times are simulated.
32 devices in a mesh: gy: 4 (over z), gx: 8 (over y, x, core).
Axes of the slice: x: 2, y: 2, z: 4, core: 2. Of those that a mesh axis runs over, the one named last changes fastest.
Arguments:
- radiance: bfloat16 [256, 256, 4096], P('gy', 'gx'), may hold values from -64 to 64
- kernel: float32 [3, 3, 4096], replicated, may hold values from 0.05 to 0.5
- test_matrix: bfloat16 [4096, 128], replicated, may hold values from -0.09375 to 0.09375
Outputs:
- basis_out: float32 [256, 256, 128], P('gy', 'gx')
- coeffs: float32 [128, 4096], replicated
All inputs are finite; a program needn't handle non-finite values.
Results may differ from a plain program's by a relative error of at most 0.00085.
The roundings to bfloat16 on the way count: a program that leaves them out, or rounds other values in their place, can miss the bound.
Values may be sent and summed in bfloat16 or wider, within the bound.
A program may use at most 192 MiB of HBM per device.

v0:
```python
import math

import jax
import jax.numpy as jnp
from jax import lax
from jax.sharding import PartitionSpec as P


def from_partner(value, axis, apart):
    mask = 2**apart
    pairs = [(source, source ^ mask) for source in range(lax.axis_size(axis))]
    return lax.ppermute(value, axis, pairs)


def with_halo(array, sides, width):
    for axis, dim in sides:
        devices, length = (lax.axis_size(axis), array.shape[dim])
        up = [(i, (i + 1) % devices) for i in range(devices - 1)]
        down = [(j, i) for i, j in up]
        last = lax.slice_in_dim(array, length - width, length, axis=dim)
        first = lax.slice_in_dim(array, 0, width, axis=dim)
        before = lax.ppermute(last, axis, up)
        after = lax.ppermute(first, axis, down)
        array = jnp.concatenate([before, array, after], axis=dim)
    return array


def smooth_block(padded, kernel, row_total, col_total):
    summed = jnp.zeros((row_total, col_total, padded.shape[2]), jnp.float32)
    for row_shift in range(3):
        for col_shift in range(3):
            window = padded[
                row_shift : row_shift + row_total, col_shift : col_shift + col_total
            ].astype(jnp.float32)
            summed = summed + kernel[row_shift, col_shift] * window
    return summed.astype(jnp.bfloat16)


def gram_of(values):
    return jnp.dot(
        values.T, values, precision=lax.Precision.HIGHEST, preferred_element_type=jnp.float32
    )


def combine_pair(triangle, partner):
    joined = jnp.dot(
        triangle, triangle.T, precision=lax.Precision.HIGHEST, preferred_element_type=jnp.float32
    )
    joined = joined + jnp.dot(
        partner, partner.T, precision=lax.Precision.HIGHEST, preferred_element_type=jnp.float32
    )
    return jnp.linalg.cholesky(joined)


def rows_levels(triangle):
    for bit_number in range(lax.axis_size("gy").bit_length() - 1):
        triangle = combine_pair(triangle, from_partner(triangle, "gy", bit_number))
    return triangle


def cols_levels(triangle):
    for bit_number in range(lax.axis_size("gx").bit_length() - 1):
        triangle = combine_pair(triangle, from_partner(triangle, "gx", bit_number))
    return triangle


def factor_basis(values):
    local_gram = gram_of(values)
    triangle = jnp.linalg.cholesky(local_gram)
    triangle = cols_levels(rows_levels(triangle))
    return lax.linalg.triangular_solve(
        triangle, values, left_side=False, lower=True, transpose_a=True
    )


def on_device(radiance, kernel, test_matrix):
    height, breadth, channels = radiance.shape
    devices = lax.axis_size("gy") * lax.axis_size("gx")
    pixel_count = height * breadth * devices
    padded = with_halo(radiance, (("gy", 0), ("gx", 1)), 1)
    smoothed = smooth_block(padded, kernel, height, breadth)
    flattened = smoothed.reshape(height * breadth, channels)
    sketch = jnp.dot(flattened, test_matrix, preferred_element_type=jnp.float32)
    first_basis = factor_basis(sketch).astype(jnp.bfloat16)
    summed = lax.psum(
        jnp.dot(first_basis.T, flattened, preferred_element_type=jnp.float32), ("gy", "gx")
    )
    range_map = summed.astype(jnp.bfloat16)
    second = jnp.dot(flattened, range_map.T, preferred_element_type=jnp.float32)
    basis_out = factor_basis(second) * math.sqrt(pixel_count)
    basis_half = basis_out.astype(jnp.bfloat16)
    projected = jnp.dot(basis_half.T, flattened, preferred_element_type=jnp.float32)
    coeffs = lax.psum(projected, ("gy", "gx")) * (math.sqrt(channels) / pixel_count)
    return (basis_out.reshape(height, breadth, basis_out.shape[1]), coeffs)


def solution(mesh):
    placed = (P("gy", "gx", None), P(), P())
    return jax.shard_map(
        on_device, mesh=mesh, in_specs=placed, out_specs=(P("gy", "gx", None), P()), check_vma=False
    )
```

profile of v0, /device:TPU:0, one launch (start us, length us, event | category | flops | bytes accessed | tf_op | source)
XLA Modules:
  0.0 596.3 jit_solution(1109659623449336028)
XLA Ops:
  7.2 1.1 fusion.59
  8.4 4.9 collective-permute-start
  13.3 1.3 collective-permute-start.1
  14.6 4.2 collective-permute-done
  18.9 8.9 %constant_dynamic-update-slice_fusion.1 = bf16[66,32,4096]{2,1,0:T(8,128)(2,1)S(1)} fusion(bf16[66,32,4096]{2,1,0:T(8,128)(2,1)S(1)} %constant_dynamic-update-slice_fusion.2, bf16[64,32,4096]{2,1,0:T(8,128)(2,1)} %param.6), kind=kLoop, calls=%fused_computation.102 | loop fusion | bytes 33554432
  27.8 0.7 copy-done.3
  28.5 5.9 copy-done.2
  34.4 2.4 fusion.58
  38.0 1.3 collective-permute-start.3
  39.3 3.1 collective-permute-start.2
  42.4 0.7 fusion.60
  43.1 1.2 copy.113
  44.3 1.2 copy.111
  45.5 71.6 %add_convert_fusion = bf16[64,32,4096]{2,1,0:T(8,128)(2,1)} fusion(bf16[64,32,4096]{2,1,0:T(8,128)(2,1)} %param.6, bf16[66,32,4096]{2,1,0:T(8,128)(2,1)} %copy-done.2, bf16[66,1,4096]{2,1,0:T(2,128)(2,1)S(1)} %copy.113, bf16[66,1,4096]{2,1,0:T(2,128)(2,1)S(1)} %copy.111, bf16[1,32,4096]{2,1,0:T(8,128)(2,1)} %copy-done.3, ...), kind=kLoop, calls=%fused_computation | loop fusion | flops 427819008 | bytes 52609024 | tf_op jit(solution)/shard_map/convert_element_type | solution.py:36
  117.2 8.3 %fusion.61 = f32[2048,128]{1,0:T(8,128)S(1)} fusion(bf16[2048,4096]{1,0:T(8,128)(2,1)} %bitcast.130, bf16[4096,128]{1,0:T(8,128)(2,1)S(1)} %copy-done), kind=kOutput, calls=%fused_computation.119 | convolution fusion | flops 2147483648 | bytes 18874368 | tf_op jit(solution)/shard_map/dot_general | solution.py:83
  125.5 1.8 fusion.62
  127.4 11.7 %cholesky.194 = f32[128,128]{1,0:T(8,128)S(1)} custom-call(f32[128,128]{1,0:T(8,128)S(1)} %fusion.25), custom_call_target="Cholesky" | custom-call | tf_op jit(solution)/shard_map/jit(cholesky)/cholesky | solution.py:69
  139.8 0.7 fusion.35
  140.5 2.5 collective-permute-start.4
  143.3 2.0 collective-permute-done.4
  145.6 11.7 %cholesky.205 = f32[128,128]{1,0:T(8,128)S(1)} custom-call(f32[128,128]{1,0:T(8,128)S(1)} %fusion.24), custom_call_target="Cholesky" | custom-call | tf_op jit(solution)/shard_map/jit(cholesky)/cholesky | solution.py:52
  158.0 0.7 fusion.29
  158.7 3.1 collective-permute-start.5
  162.1 2.0 collective-permute-done.5
  164.4 11.9 %cholesky.216 = f32[128,128]{1,0:T(8,128)S(1)} custom-call(f32[128,128]{1,0:T(8,128)S(1)} %fusion.23), custom_call_target="Cholesky" | custom-call | tf_op jit(solution)/shard_map/jit(cholesky)/cholesky | solution.py:52
  177.0 0.7 fusion.26
  177.7 7.4 %collective-permute-start.6 = (f32[128,128]{1,0:T(8,128)S(1)}, f32[128,128]{1,0:T(8,128)S(1)}, u32[]{:S(2)}, u32[]{:S(2)}) collective-permute-start(f32[128,128]{1,0:T(8,128)S(1)} %fusion.26), channel_id=1, source_target_pairs={{0,1},{1,0},{2,3},{3,2},{4,5},{5,4},{6,7},{7,6},{8,9},{9,8},{10,11... | collective-permute-start | bytes 196616 | tf_op jit(solution)/shard_map/ppermute | solution.py:12
  186.4 11.7 %cholesky.227 = f32[128,128]{1,0:T(8,128)S(1)} custom-call(f32[128,128]{1,0:T(8,128)S(1)} %fusion.22), custom_call_target="Cholesky" | custom-call | tf_op jit(solution)/shard_map/jit(cholesky)/cholesky | solution.py:52
  198.8 0.7 fusion.27
  199.4 4.2 collective-permute-start.7
  203.9 2.2 collective-permute-done.7
  206.5 11.7 %cholesky.238 = f32[128,128]{1,0:T(8,128)S(1)} custom-call(f32[128,128]{1,0:T(8,128)S(1)} %fusion.21), custom_call_target="Cholesky" | custom-call | tf_op jit(solution)/shard_map/jit(cholesky)/cholesky | solution.py:52
  219.5 3.5 collective-permute-start.8
  223.2 2.0 collective-permute-done.8
  225.6 12.1 %cholesky.249 = f32[128,128]{1,0:T(8,128)S(1)} custom-call(f32[128,128]{1,0:T(8,128)S(1)} %fusion.20), custom_call_target="Cholesky" | custom-call | tf_op jit(solution)/shard_map/jit(cholesky)/cholesky | solution.py:52
  238.4 0.7 fusion.10
  239.1 9.8 %custom-call.6 = f32[1,128,128]{1,2,0:T(8,128)S(1)} custom-call(f32[1,128,128]{2,1,0:T(8,128)S(1)} %fusion.10), custom_call_target="InvertDiagBlocksLowerTriangular" | custom-call | tf_op jit(solution)/shard_map/triangular_solve/custom-call.0 | solution.py:71
  248.9 1.1 fusion.5
  250.0 8.1 %fusion.68 = f32[128,4096]{1,0:T(8,128)S(1)} fusion(bf16[2048,128]{0,1:T(8,128)(2,1)S(1)} %fusion.5, bf16[2048,4096]{1,0:T(8,128)(2,1)} %bitcast.131), kind=kOutput, calls=%fused_computation.126 | convolution fusion | flops 2147483648 | bytes 19398656 | tf_op jit(solution)/shard_map/dot_general | solution.py:86
  258.1 64.0 %all-reduce.4 = bf16[128,4096]{1,0:T(8,128)(2,1)S(1)} all-reduce(f32[128,4096]{1,0:T(8,128)S(1)} %fusion.68), channel_id=1, replica_groups=mesh['gy'=4,'gx'=8] {'gy','gx'}, use_global_device_ids=true, to_apply=%region_2.5 | all-reduce | flops 524288 | bytes 3145728 | tf_op jit(solution)/shard_map/psum | solution.py:85
  322.0 8.3 %fusion.75 = f32[2048,128]{1,0:T(8,128)S(1)} fusion(bf16[2048,4096]{1,0:T(8,128)(2,1)} %bitcast.132, bf16[128,4096]{1,0:T(8,128)(2,1)S(1)} %all-reduce.4), kind=kOutput, calls=%fused_computation.133 | convolution fusion | flops 2147483648 | bytes 18874368 | tf_op jit(solution)/shard_map/dot_general | solution.py:89
  330.3 1.8 fusion.69
  332.3 11.7 %cholesky.260 = f32[128,128]{1,0:T(8,128)S(1)} custom-call(f32[128,128]{1,0:T(8,128)S(1)} %fusion.18), custom_call_target="Cholesky" | custom-call | tf_op jit(solution)/shard_map/jit(cholesky)/cholesky | solution.py:69
  345.3 2.1 collective-permute-start.9
  347.7 2.0 collective-permute-done.9
  350.1 11.7 %cholesky.271 = f32[128,128]{1,0:T(8,128)S(1)} custom-call(f32[128,128]{1,0:T(8,128)S(1)} %fusion.17), custom_call_target="Cholesky" | custom-call | tf_op jit(solution)/shard_map/jit(cholesky)/cholesky | solution.py:52
  363.2 2.4 collective-permute-start.10
  365.8 2.5 collective-permute-done.10
  368.8 11.9 %cholesky.282 = f32[128,128]{1,0:T(8,128)S(1)} custom-call(f32[128,128]{1,0:T(8,128)S(1)} %fusion.16), custom_call_target="Cholesky" | custom-call | tf_op jit(solution)/shard_map/jit(cholesky)/cholesky | solution.py:52
  382.3 1.0 collective-permute-done.11
  383.7 11.7 %cholesky.293 = f32[128,128]{1,0:T(8,128)S(1)} custom-call(f32[128,128]{1,0:T(8,128)S(1)} %fusion.15), custom_call_target="Cholesky" | custom-call | tf_op jit(solution)/shard_map/jit(cholesky)/cholesky | solution.py:52
  396.8 1.0 collective-permute-start.12
  398.0 3.1 collective-permute-done.12
  401.5 11.7 %cholesky.304 = f32[128,128]{1,0:T(8,128)S(1)} custom-call(f32[128,128]{1,0:T(8,128)S(1)} %fusion.14), custom_call_target="Cholesky" | custom-call | tf_op jit(solution)/shard_map/jit(cholesky)/cholesky | solution.py:52
  414.5 1.0 collective-permute-start.13
  415.8 3.1 collective-permute-done.13
  419.2 12.0 %cholesky.315 = f32[128,128]{1,0:T(8,128)S(1)} custom-call(f32[128,128]{1,0:T(8,128)S(1)} %fusion.13), custom_call_target="Cholesky" | custom-call | tf_op jit(solution)/shard_map/jit(cholesky)/cholesky | solution.py:52
  431.9 0.7 fusion.11
  432.6 9.8 %custom-call.7 = f32[1,128,128]{1,2,0:T(8,128)S(1)} custom-call(f32[1,128,128]{2,1,0:T(8,128)S(1)} %fusion.11), custom_call_target="InvertDiagBlocksLowerTriangular" | custom-call | tf_op jit(solution)/shard_map/triangular_solve/custom-call.0 | solution.py:71
  442.4 1.1 fusion.4
  443.5 9.4 %fusion.8 = f32[128,4096]{1,0:T(8,128)} fusion(bf16[2048,4096]{1,0:T(8,128)(2,1)} %bitcast.133, f32[2048,128]{0,1:T(8,128)S(1)} %fusion.4), kind=kOutput, calls=%fused_computation.34 | convolution fusion | flops 2147745792 | bytes 19922944 | tf_op jit(solution)/shard_map/dot_general | solution.py:92
  452.9 1.3 copy.146
  454.2 131.7 %all-reduce.3.cloned.1.call-done = f32[128,4096]{1,0:T(8,128)} async-done(((f32[128,4096]{1,0:T(8,128)}), f32[128,4096]{1,0:T(8,128)}) %all-reduce.3.cloned.1.call-update) | async-done | bytes 2097168 | tf_op jit(solution)/shard_map/psum | solution.py:93
  585.9 3.1 broadcast_multiply_fusion
  (93 shorter events, 20.6 us)
Async XLA Ops:
  7.2 110.0 %copy-start = (bf16[4096,128]{1,0:T(8,128)(2,1)S(1)}, bf16[4096,128]{1,0:T(8,128)(2,1)}, u32[]{:S(2)}) copy-start(bf16[4096,128]{1,0:T(8,128)(2,1)} %param.8) | copy-start | bytes 3145732
  7.2 578.7 %all-reduce.3.cloned.1.call-start = ((), (), s32[]{:S(2)}) async-start(), calls=%async_computation | async-start | bytes 4194304 | tf_op jit(solution)/shard_map/psum | solution.py:93
  8.4 10.5 %collective-permute-start = (bf16[1,32,4096]{2,1,0:T(8,128)(2,1)S(1)}, bf16[1,32,4096]{2,1,0:T(8,128)(2,1)S(1)}, u32[]{:S(2)}, u32[]{:S(2)}) collective-permute-start(bf16[1,32,4096]{2,1,0:T(8,128)(2,1)S(1)} %get-tuple-element.9), channel_id=1, source_target_pairs={{0,8},{8,16},{16,24},{1,9},{9,17},{17,25},{2,10},{10,18},{18,26},{... | collective-permute-start | bytes 786440 | tf_op jit(solution)/shard_map/ppermute | solution.py:22
  13.3 14.5 %collective-permute-start.1 = (bf16[1,32,4096]{2,1,0:T(8,128)(2,1)S(1)}, bf16[1,32,4096]{2,1,0:T(8,128)(2,1)S(1)}, u32[]{:S(2)}, u32[]{:S(2)}) collective-permute-start(bf16[1,32,4096]{2,1,0:T(8,128)(2,1)S(1)} %get-tuple-element.8), channel_id=1, source_target_pairs={{8,0},{16,8},{24,16},{9,1},{17,9},{25,17},{10,2},{18,10},{26,18},{... | collective-permute-start | bytes 786440 | tf_op jit(solution)/shard_map/ppermute | solution.py:23
  18.9 23.5 %copy-start.4 = (f32[3,3,4096]{2,1,0:T(4,128)S(1)}, f32[3,3,4096]{2,1,0:T(4,128)}, u32[]{:S(2)}) copy-start(f32[3,3,4096]{2,1,0:T(4,128)} %param.7) | copy-start | bytes 442372
  27.8 0.7 copy-start.3
  28.5 5.9 copy-start.2
  38.0 5.1 collective-permute-start.3
  39.3 5.0 collective-permute-start.2
  140.5 4.8 collective-permute-start.4
  158.7 5.3 collective-permute-start.5
  177.7 8.3 %collective-permute-start.6 = (f32[128,128]{1,0:T(8,128)S(1)}, f32[128,128]{1,0:T(8,128)S(1)}, u32[]{:S(2)}, u32[]{:S(2)}) collective-permute-start(f32[128,128]{1,0:T(8,128)S(1)} %fusion.26), channel_id=1, source_target_pairs={{0,1},{1,0},{2,3},{3,2},{4,5},{5,4},{6,7},{7,6},{8,9},{9,8},{10,11... | collective-permute-start | bytes 196616 | tf_op jit(solution)/shard_map/ppermute | solution.py:12
  199.4 6.7 %collective-permute-start.7 = (f32[128,128]{1,0:T(8,128)S(1)}, f32[128,128]{1,0:T(8,128)S(1)}, u32[]{:S(2)}, u32[]{:S(2)}) collective-permute-start(f32[128,128]{1,0:T(8,128)S(1)} %fusion.27), channel_id=1, source_target_pairs={{0,2},{1,3},{2,0},{3,1},{4,6},{5,7},{6,4},{7,5},{8,10},{9,11},{10,... | collective-permute-start | bytes 196616 | tf_op jit(solution)/shard_map/ppermute | solution.py:12
  219.5 5.7 collective-permute-start.8
  345.3 4.4 collective-permute-start.9
  363.2 5.2 collective-permute-start.10
  382.0 1.3 collective-permute-start.11
  396.8 4.3 collective-permute-start.12
  414.5 4.3 collective-permute-start.13
  432.5 156.4 %copy-start.1 = (bf16[4096,128]{1,0:T(8,128)(2,1)S(1)}, bf16[4096,128]{1,0:T(8,128)(2,1)}, u32[]{:S(2)}) copy-start(bf16[4096,128]{1,0:T(8,128)(2,1)} %param.8) | copy-start | bytes 3145732
Sparse Core Ops, SparseCore 0:
  453.0 132.8 all-reduce.2
where the time goes:
time: 605 us; the launch traced here: 596 us
  other arithmetic  252 us (42%)
  waiting for transfers between devices  156 us (26%)
  blocking collectives  64 us (11%)
  matrix products  45.2 us (7%)
  starting transfers between devices  38 us (6%)
  local copies, waits for them, and re-layouts  25.8 us (4%)
  between operations  15 us (2%)
    psum x1, waiting for transfers between devices, on_device(): lax.psum(projected, ('gy', 'gx')) * (math.sqrt(channels) / pixel_count)  132 us
    another operation x30, other arithmetic, combine_pair(): return jnp.linalg.cholesky(joined)  125 us
    convert_element_type x1, other arithmetic, smooth_block(): return summed.astype(jnp.bfloat16)  71.6 us
    psum x1, blocking collectives, on_device(): lax.psum(jnp.dot(first_basis.T, flattened, preferred_element_type=jnp.flo...  64 us
    ppermute x10, starting transfers between devices, from_partner(): return lax.ppermute(value, axis, pairs)  27.4 us
    another operation x6, other arithmetic, factor_basis(): triangle = jnp.linalg.cholesky(local_gram)  24.8 us
    another operation x4, other arithmetic, factor_basis(): lax.linalg.triangular_solve(triangle, values, left_side=False, lower=True...  20.9 us
    ppermute x10, waiting for transfers between devices, from_partner(): return lax.ppermute(value, axis, pairs)  20.4 us
  transfers between devices with their start and end apart: 15, of which 12 were waited for; matrix products, arithmetic and copies ran while one was open for 2% of the time, Pallas kernels for 0%

commit v1 on v0

v1 whole, which is shorter than its diff:
```python
import functools
import math

import jax
import jax.numpy as jnp
from jax import lax
from jax.experimental import pallas as pl
from jax.experimental.pallas import tpu as pltpu
from jax.sharding import PartitionSpec as P

MESH = pl.DeviceIdType.MESH
LANES = 128
VMEM_LIMIT = 56 * 1024 * 1024


def bit_of(index, bit):
    return (index // 2**bit) % 2


def flipped(index, mask, bits):
    for bit in range(bits):
        if (mask >> bit) & 1:
            index = index + 2**bit * (1 - 2 * bit_of(index, bit))
    return index


def greet(partners):
    barrier = pltpu.get_barrier_semaphore()
    for partner in partners:
        pl.semaphore_signal(barrier, inc=1, device_id=partner, device_id_type=MESH)
    pl.semaphore_wait(barrier, len(partners))


def shifted_pairs(rows, cols, n_gy, n_gx):
    pairs = []
    for y in range(n_gy):
        for x in range(n_gx):
            if 0 <= y + rows < n_gy and 0 <= x + cols < n_gx:
                pairs.append((y * n_gx + x, (y + rows) * n_gx + x + cols))
    return pairs


def smooth_kernel(x_ref, up_ref, down_ref, left_ref, right_ref, k_ref, t_ref, o_ref, s_ref, l_s, r_s):
    height, width, block = x_ref.shape

    @pl.when(pl.program_id(0) == 0)
    def _():
        s_ref[...] = jnp.zeros_like(s_ref)

    for part in range(block // LANES):
        lanes = pl.ds(part * LANES, LANES)
        left = left_ref[:, lanes].astype(jnp.float32)
        right = right_ref[:, lanes].astype(jnp.float32)
        k = [[k_ref[pl.ds(3 * a + b, 1), lanes] for b in range(3)] for a in range(3)]
        l_s[...] = sum(k[a][0] * left[a : a + height] for a in range(3))
        r_s[...] = sum(k[a][2] * right[a : a + height] for a in range(3))
        place = lax.broadcasted_iota(jnp.int32, (width, LANES), 0)

        def row_out(h, above, here, below):
            p = [k[0][b] * above + k[1][b] * here + k[2][b] * below for b in range(3)]
            before = jnp.where(place == 0, l_s[pl.ds(h, 1), :], pltpu.roll(p[0], 1, 0))
            after = jnp.where(place == width - 1, r_s[pl.ds(h, 1), :], pltpu.roll(p[2], width - 1, 0))
            o_ref[h, :, lanes] = (p[1] + before + after).astype(jnp.bfloat16)

        def step(h, carry):
            above, here = carry
            below = x_ref[h + 1, :, lanes].astype(jnp.float32)
            row_out(h, above, here, below)
            return here, below

        first = (up_ref[:, lanes].astype(jnp.float32), x_ref[0, :, lanes].astype(jnp.float32))
        above, here = lax.fori_loop(0, height - 1, step, first, unroll=3)
        row_out(height - 1, above, here, down_ref[:, lanes].astype(jnp.float32))

    s_ref[...] += jnp.dot(
        o_ref[...].reshape(height * width, block), t_ref[...], preferred_element_type=jnp.float32
    )


def smooth_and_sketch(radiance, kernel, test_matrix):
    height, width, channels = radiance.shape
    k_width = test_matrix.shape[1]
    n_gy, n_gx = lax.axis_size("gy"), lax.axis_size("gx")
    block = 512

    def moved(value, rows, cols):
        return lax.ppermute(value, ("gy", "gx"), shifted_pairs(rows, cols, n_gy, n_gx))

    up = moved(radiance[height - 1], 1, 0)
    down = moved(radiance[0], -1, 0)
    sides = []
    for cols, place in ((1, width - 1), (-1, 0)):
        middle = moved(radiance[:, place], 0, cols)
        top = moved(radiance[height - 1 :, place], 1, cols)
        bottom = moved(radiance[:1, place], -1, cols)
        sides.append(jnp.concatenate([top, middle, bottom], axis=0))
    pixels = height * width
    return pl.pallas_call(
        smooth_kernel,
        grid=(channels // block,),
        in_specs=[
            pl.BlockSpec((height, width, block), lambda i: (0, 0, i)),
            pl.BlockSpec((width, block), lambda i: (0, i)),
            pl.BlockSpec((width, block), lambda i: (0, i)),
            pl.BlockSpec((height + 2, block), lambda i: (0, i)),
            pl.BlockSpec((height + 2, block), lambda i: (0, i)),
            pl.BlockSpec((9, block), lambda i: (0, i)),
            pl.BlockSpec((block, k_width), lambda i: (i, 0)),
        ],
        out_specs=[
            pl.BlockSpec((height, width, block), lambda i: (0, 0, i)),
            pl.BlockSpec((pixels, k_width), lambda i: (0, 0)),
        ],
        out_shape=[
            jax.ShapeDtypeStruct((height, width, channels), jnp.bfloat16),
            jax.ShapeDtypeStruct((pixels, k_width), jnp.float32),
        ],
        scratch_shapes=[
            pltpu.VMEM((height, LANES), jnp.float32),
            pltpu.VMEM((height, LANES), jnp.float32),
        ],
        compiler_params=pltpu.CompilerParams(vmem_limit_bytes=VMEM_LIMIT),
        cost_estimate=pl.CostEstimate(
            flops=pixels * channels * (2 * k_width + 18),
            bytes_accessed=4 * pixels * channels,
            transcendentals=0,
        ),
        name="smooth_sketch",
    )(radiance, up, down, sides[0], sides[1], kernel.reshape(9, channels), test_matrix)


def tree_sum(values):
    while len(values) > 1:
        values = [values[i] + values[i + 1] for i in range(0, len(values), 2)]
    return values[0]


def gram_kernel(n_gy, n_gx, x_ref, o_ref, recv_x, recv_y, mine, sx, rx, sy, ry, sg, rg):
    bits_x, bits_y = n_gx.bit_length() - 1, n_gy.bit_length() - 1
    me_x, me_y = lax.axis_index("gx"), lax.axis_index("gy")
    rows = x_ref.shape[0] // n_gx
    along_x = [flipped(me_x, d, bits_x) for d in range(n_gx)]
    along_y = [flipped(me_y, d, bits_y) for d in range(n_gy)]
    greet([(me_y, p) for p in along_x[1:]] + [(p, me_x) for p in along_y[1:]])

    def block(ref, index):
        return ref.at[pl.ds(pl.multiple_of(index * rows, rows), rows), :]

    copies = []
    for d in range(1, n_gx):
        copy = pltpu.make_async_remote_copy(
            block(x_ref, along_x[d]), recv_x.at[d], sx.at[d], rx.at[d], (me_y, along_x[d]), MESH
        )
        copy.start()
        copies.append(copy)
    for copy in copies:
        copy.wait_recv()
    own = x_ref[pl.ds(pl.multiple_of(me_x * rows, rows), rows), :]
    mine[...] = tree_sum([own] + [recv_x[d] for d in range(1, n_gx)])
    later = []
    for d in range(1, n_gy):
        copy = pltpu.make_async_remote_copy(
            mine, recv_y.at[d], sy.at[d], ry.at[d], (along_y[d], me_x), MESH
        )
        copy.start()
        later.append(copy)
    for copy in later:
        copy.wait_recv()
    total = tree_sum([mine[...]] + [recv_y[d] for d in range(1, n_gy)])
    o_ref[pl.ds(pl.multiple_of(me_x * rows, rows), rows), :] = total
    last = []
    for d in range(1, n_gx):
        copy = pltpu.make_async_remote_copy(
            block(o_ref, me_x), block(o_ref, me_x), sg.at[d], rg.at[d], (me_y, along_x[d]), MESH
        )
        copy.start()
        last.append(copy)
    for d in range(1, n_gx):
        pltpu.make_async_remote_copy(
            block(o_ref, along_x[d]), block(o_ref, along_x[d]), sg.at[d], rg.at[d], (me_y, along_x[d]), MESH
        ).wait_recv()
    for copy in copies + later + last:
        copy.wait_send()


def summed_gram(gram, collective_id):
    n_gy, n_gx = lax.axis_size("gy"), lax.axis_size("gx")
    k = gram.shape[0]
    rows = k // n_gx
    dma = pltpu.SemaphoreType.DMA
    return pl.pallas_call(
        functools.partial(gram_kernel, n_gy, n_gx),
        out_shape=jax.ShapeDtypeStruct(gram.shape, jnp.float32),
        in_specs=[pl.BlockSpec(memory_space=pltpu.VMEM)],
        out_specs=pl.BlockSpec(memory_space=pltpu.VMEM),
        scratch_shapes=[
            pltpu.VMEM((n_gx, rows, k), jnp.float32),
            pltpu.VMEM((n_gy, rows, k), jnp.float32),
            pltpu.VMEM((rows, k), jnp.float32),
            dma((n_gx,)),
            dma((n_gx,)),
            dma((n_gy,)),
            dma((n_gy,)),
            dma((n_gx,)),
            dma((n_gx,)),
        ],
        compiler_params=pltpu.CompilerParams(collective_id=collective_id, has_side_effects=True),
        name="gram_sum",
    )(gram)


def wide_orders(n_gy, n_gx):
    x_bits = [("gx", b) for b in range(n_gx.bit_length() - 1)]
    y_bits = [("gy", b) for b in range(n_gy.bit_length() - 1)]
    first, across = x_bits[:1], x_bits[1:]
    return [first + across + y_bits, first + across[::-1] + y_bits]


def halvings(rows, cols, count):
    shapes = []
    for _ in range(count):
        if rows > 16:
            rows //= 2
        else:
            cols //= 2
        shapes.append((rows, cols))
    return shapes


def wide_kernel(orders, x_ref, o_ref, *scratch):
    steps, chunks = len(orders[0]), len(orders)
    rows, cols = x_ref.shape
    wide = cols // chunks
    work = scratch[0]
    recv = [scratch[1 + q * steps : 1 + (q + 1) * steps] for q in range(chunks)]
    s_send, s_recv, g_send, g_recv = scratch[1 + chunks * steps :]
    me = {"gx": lax.axis_index("gx"), "gy": lax.axis_index("gy")}

    def partner(axis, bit):
        other = dict(me)
        other[axis] = flipped(me[axis], 1 << bit, bit + 1)
        return (other["gy"], other["gx"])

    greet([partner(*which) for which in orders[0]])
    shapes = halvings(rows, wide, steps)
    kept, sent = [], []
    for q in range(chunks):
        row, col = 0, q * wide
        size = (rows, wide)
        kept_q, sent_q = [], []
        for s, (axis, bit) in enumerate(orders[q]):
            mine = bit_of(me[axis], bit)
            h, w = shapes[s]
            if h < size[0]:
                kept_q.append((row + mine * h, col))
                sent_q.append((row + (1 - mine) * h, col))
            else:
                kept_q.append((row, col + mine * w))
                sent_q.append((row, col + (1 - mine) * w))
            row, col = kept_q[-1]
            size = (h, w)
        kept.append(kept_q)
        sent.append(sent_q)

    def region(place, shape):
        row = place[0] if isinstance(place[0], int) else pl.multiple_of(place[0], 16)
        col = place[1] if isinstance(place[1], int) else pl.multiple_of(place[1], LANES)
        return (pl.ds(row, shape[0]), pl.ds(col, shape[1]))

    def reduce_copy(q, s):
        source = x_ref if s == 0 else work
        return pltpu.make_async_remote_copy(
            source.at[region(sent[q][s], shapes[s])],
            recv[q][s],
            s_send.at[q * steps + s],
            s_recv.at[q * steps + s],
            partner(*orders[q][s]),
            MESH,
        )

    def gather_copy(q, s, outgoing):
        place = region(kept[q][s] if outgoing else sent[q][s], shapes[s])
        return pltpu.make_async_remote_copy(
            o_ref.at[place],
            o_ref.at[place],
            g_send.at[q * steps + s],
            g_recv.at[q * steps + s],
            partner(*orders[q][s]),
            MESH,
        )

    for q in range(chunks):
        reduce_copy(q, 0).start()
    for s in range(steps):
        for q in range(chunks):
            reduce_copy(q, s).wait_recv()
            here = region(kept[q][s], shapes[s])
            source = x_ref if s == 0 else work
            total = source[here] + recv[q][s][...]
            if s + 1 < steps:
                work[here] = total
                reduce_copy(q, s + 1).start()
            else:
                o_ref[here] = total.astype(o_ref.dtype)
                gather_copy(q, s, True).start()
    for s in reversed(range(steps)):
        for q in range(chunks):
            gather_copy(q, s, False).wait_recv()
            if s > 0:
                gather_copy(q, s - 1, True).start()
    for s in range(steps):
        for q in range(chunks):
            reduce_copy(q, s).wait_send()
            gather_copy(q, s, True).wait_send()


def summed_wide(values, dtype, collective_id):
    n_gy, n_gx = lax.axis_size("gy"), lax.axis_size("gx")
    orders = wide_orders(n_gy, n_gx)
    rows, cols = values.shape
    steps, chunks = len(orders[0]), len(orders)
    shapes = halvings(rows, cols // chunks, steps)
    dma = pltpu.SemaphoreType.DMA((chunks * steps,))
    return pl.pallas_call(
        functools.partial(wide_kernel, orders),
        out_shape=jax.ShapeDtypeStruct(values.shape, dtype),
        in_specs=[pl.BlockSpec(memory_space=pltpu.VMEM)],
        out_specs=pl.BlockSpec(memory_space=pltpu.VMEM),
        scratch_shapes=[pltpu.VMEM((rows, cols), jnp.float32)]
        + [pltpu.VMEM(shape, jnp.float32) for _ in range(chunks) for shape in shapes]
        + [dma] * 4,
        compiler_params=pltpu.CompilerParams(
            collective_id=collective_id, has_side_effects=True, vmem_limit_bytes=VMEM_LIMIT
        ),
        name="wide_sum",
    )(values)


def factor_basis(values, collective_id):
    local_gram = jnp.dot(
        values.T, values, precision=lax.Precision.HIGHEST, preferred_element_type=jnp.float32
    )
    triangle = jnp.linalg.cholesky(summed_gram(local_gram, collective_id))
    return lax.linalg.triangular_solve(
        triangle, values, left_side=False, lower=True, transpose_a=True
    )


def on_device(radiance, kernel, test_matrix):
    height, breadth, channels = radiance.shape
    devices = lax.axis_size("gy") * lax.axis_size("gx")
    pixel_count = height * breadth * devices
    smoothed, sketch = smooth_and_sketch(radiance, kernel, test_matrix)
    flattened = smoothed.reshape(height * breadth, channels)
    first_basis = factor_basis(sketch, 0).astype(jnp.bfloat16)
    range_map = summed_wide(
        jnp.dot(first_basis.T, flattened, preferred_element_type=jnp.float32), jnp.bfloat16, 2
    )
    second = jnp.dot(flattened, range_map.T, preferred_element_type=jnp.float32)
    basis_out = factor_basis(second, 1) * math.sqrt(pixel_count)
    basis_half = basis_out.astype(jnp.bfloat16)
    projected = jnp.dot(basis_half.T, flattened, preferred_element_type=jnp.float32)
    coeffs = summed_wide(projected, jnp.float32, 3) * (math.sqrt(channels) / pixel_count)
    return (basis_out.reshape(height, breadth, basis_out.shape[1]), coeffs)


def solution(mesh):
    placed = (P("gy", "gx", None), P(), P())
    return jax.shard_map(
        on_device, mesh=mesh, in_specs=placed, out_specs=(P("gy", "gx", None), P()), check_vma=False
    )
```

time: 605 us -> 289 us (0.48); the launches traced: 596 us -> 288 us
  other arithmetic: 252 us -> 52.5 us
  Pallas kernels: 0 us -> 161 us
  waiting for transfers between devices: 156 us -> 2.97 us
  blocking collectives: 64 us -> 0 us
  starting transfers between devices: 38 us -> 21.9 us
  between operations: 15 us -> 0.89 us
  local copies, waits for them, and re-layouts: 25.8 us -> 12.5 us
  matrix products: 45.2 us -> 36.2 us
    pallas_call x0 -> x5, Pallas kernels: none -> 161 us  [the longest x2 88.1 us: summed_wide(): pl.pallas_call(functools.partial(wide_kernel, orders), out_shape=jax.Shap...]
    psum x1 -> x0, waiting for transfers between devices: 132 us -> none  [on_device(): lax.psum(projected, ('gy', 'gx')) * (math.sqrt(channels) / pixel_count)]
    another operation x36 -> x6, other arithmetic: 150 us -> 24.8 us  [factor_basis(): triangle = jnp.linalg.cholesky(summed_gram(local_gram, collective_id))]
    convert_element_type x1 -> x0, other arithmetic: 71.6 us -> none  [smooth_block(): return summed.astype(jnp.bfloat16)]
    psum x1 -> x0, blocking collectives: 64 us -> none  [on_device(): lax.psum(jnp.dot(first_basis.T, flattened, preferred_element_type=jnp.flo...]
    ppermute x14 -> x8, waiting for transfers between devices: 24.7 us -> 2.97 us  [moved(): lax.ppermute(value, ('gy', 'gx'), shifted_pairs(rows, cols, n_gy, n_gx))]
    ppermute x14 -> x8, starting transfers between devices: 37.9 us -> 21.9 us  [moved(): lax.ppermute(value, ('gy', 'gx'), shifted_pairs(rows, cols, n_gy, n_gx))]
    unnamed x12 -> x10, local copies, waits for them, and re-layouts: 15.5 us -> 1.87 us
  transfers between devices with their start and end apart: 15 -> 8, of which waited for: 12 -> 2; matrix products, arithmetic and copies ran while one was open for 2% -> 3% of each run, Pallas kernels for 0% -> 0%
where the time goes in v1:
time: 289 us; the launch traced here: 288 us
  Pallas kernels  161 us (56%)
  other arithmetic  52.5 us (18%)
  matrix products  36.2 us (13%)
  starting transfers between devices  21.9 us (8%)
  local copies, waits for them, and re-layouts  12.5 us (4%)
  waiting for transfers between devices  2.97 us (1%)
    pallas_call x2, Pallas kernels, summed_wide(): pl.pallas_call(functools.partial(wide_kernel, orders), out_shape=jax.Shap...  88.1 us
    pallas_call x1, Pallas kernels, smooth_and_sketch(): pl.pallas_call(smooth_kernel, grid=(channels // block,), in_specs=[pl.Blo...  38.6 us
    pallas_call x2, Pallas kernels, summed_gram(): pl.pallas_call(functools.partial(gram_kernel, n_gy, n_gx), out_shape=jax....  34.4 us
    another operation x6, other arithmetic, factor_basis(): triangle = jnp.linalg.cholesky(summed_gram(local_gram, collective_id))  24.8 us
    ppermute x8, starting transfers between devices, moved(): lax.ppermute(value, ('gy', 'gx'), shifted_pairs(rows, cols, n_gy, n_gx))  21.9 us
    another operation x4, other arithmetic, factor_basis(): lax.linalg.triangular_solve(triangle, values, left_side=False, lower=True...  20.9 us
    dot_general x1, matrix products, on_device(): jnp.dot(first_basis.T, flattened, preferred_element_type=jnp.float32)  9.46 us
    dot_general x1, matrix products, on_device(): jnp.dot(basis_half.T, flattened, preferred_element_type=jnp.float32)  9.43 us
  transfers between devices with their start and end apart: 8, of which 2 were waited for; matrix products, arithmetic and copies ran while one was open for 3% of the time, Pallas kernels for 0%

profile of v1, /device:TPU:0, one launch (start us, length us, event | category | flops | bytes accessed | tf_op | source)
XLA Modules:
  0.0 288.1 jit_solution(8937672165845736698)
XLA Ops:
  0.6 1.0 slice_bitcast_fusion.3
  1.6 0.7 collective-permute-start.5
  2.3 0.7 collective-permute-start.4
  3.0 9.5 %collective-permute-start.2 = (bf16[1,4096]{1,0:T(2,128)(2,1)S(1)}, bf16[1,4096]{1,0:T(2,128)(2,1)S(1)}, u32[]{:S(2)}, u32[]{:S(2)}) collective-permute-start(bf16[1,4096]{1,0:T(2,128)(2,1)S(1)} %get-tuple-element.12), channel_id=1, source_target_pairs={{0,9},{1,10},{2,11},{3,12},{4,13},{5,14},{6,15},{8,17},{9,18},{10,... | collective-permute-start | bytes 24584 | tf_op jit(solution)/shard_map/ppermute | solution.py:87
  12.5 4.6 %fusion.12 = (bf16[64,1,4096]{2,1,0:T(2,128)(2,1)S(1)}, bf16[64,1,4096]{2,1,0:T(2,128)(2,1)S(1)}) fusion(bf16[64,32,4096]{2,1,0:T(8,128)(2,1)} %x_ref.1), kind=kLoop, calls=%fused_computation.34 | loop fusion | bytes 2097152 | tf_op jit(solution)/shard_map/slice | solution.py:93
  17.1 0.0 copy-start.3
  17.1 0.6 copy.20
  17.7 2.6 collective-permute-start.3
  20.3 0.6 copy.19
  20.9 1.3 collective-permute-start.6
  22.2 1.1 slice_bitcast_fusion
  23.3 0.0 copy-done.3
  23.3 0.8 reshape.24.k_ref
  24.1 0.0 collective-permute-done.4
  24.1 1.3 collective-permute-start.7
  25.4 0.0 collective-permute-done.2
  25.4 1.3 collective-permute-start.1
  26.7 0.0 collective-permute-done.3
  26.7 4.6 %collective-permute-start = (bf16[32,4096]{1,0:T(8,128)(2,1)S(1)}, bf16[32,4096]{1,0:T(8,128)(2,1)S(1)}, u32[]{:S(2)}, u32[]{:S(2)}) collective-permute-start(bf16[32,4096]{1,0:T(8,128)(2,1)S(1)} %get-tuple-element.17), channel_id=1, source_target_pairs={{0,8},{1,9},{2,10},{3,11},{4,12},{5,13},{6,14},{7,15},{8,16},{9,17... | collective-permute-start | bytes 786440 | tf_op jit(solution)/shard_map/ppermute | solution.py:87
  31.3 1.0 pad_maximum_fusion.left_ref
  32.3 0.0 collective-permute-done.5
  32.3 0.0 collective-permute-done.7
  32.3 0.0 collective-permute-done.6
  32.3 1.0 pad_maximum_fusion.1.right_ref
  33.3 1.5 collective-permute-done.1.down_ref
  34.8 0.0 copy-start.1
  34.8 1.5 collective-permute-done.up_ref
  36.2 0.0 copy-done.1
  36.2 0.0 copy-start.2
  36.2 0.7 copy-done.2
  36.9 38.6 %smooth_sketch.1 = (bf16[64,32,4096]{2,1,0:T(8,128)(2,1)}, f32[2048,128]{1,0:T(8,128)}) custom-call(bf16[64,32,4096]{2,1,0:T(8,128)(2,1)} %x_ref.1, bf16[32,4096]{1,0:T(8,128)(2,1)} %copy-done.2, bf16[32,4096]{1,0:T(8,128)(2,1)} %copy-done.1, bf16[66,4096]{1,0:T(8,128)(2,1)} %pad_maximum_fusion.left_ref, bf16[66,4096]{1,0:T(8,128)(2,1)} %pad_maximum_fusion.1.right_ref, ...), custom_call_target="tpu_custom_call" | custom-call | flops 2298478592 | bytes 33554432 | tf_op jit(solution)/shard_map/smooth_sketch/pallas_call | solution.py:98
  75.5 0.0 copy-start
  75.5 4.1 %fusion.13.x_ref = f32[128,128]{1,0:T(8,128)} fusion(f32[2048,128]{1,0:T(8,128)} %get-tuple-element.7), kind=kOutput, calls=%fused_computation.35 | convolution fusion | flops 402653184 | bytes 1114112 | tf_op jit(solution)/shard_map/dot_general | solution.py:340
  79.6 20.4 %gram_sum.2 = f32[128,128]{1,0:T(8,128)} custom-call(f32[128,128]{1,0:T(8,128)} %fusion.13.x_ref), custom_call_target="tpu_custom_call" | custom-call | tf_op jit(solution)/shard_map/gram_sum/pallas_call | solution.py:191
  100.0 0.9 copy.12
  101.0 0.9 fusion.9
  101.8 11.7 %cholesky.44 = f32[128,128]{1,0:T(8,128)S(1)} custom-call(f32[128,128]{1,0:T(8,128)S(1)} %fusion.9), custom_call_target="Cholesky" | custom-call | tf_op jit(solution)/shard_map/jit(cholesky)/cholesky | solution.py:343
  113.6 0.6 compare_reduce_fusion.1
  114.2 0.7 fusion.4
  114.9 9.8 %custom-call.6 = f32[1,128,128]{1,2,0:T(8,128)S(1)} custom-call(f32[1,128,128]{2,1,0:T(8,128)S(1)} %fusion.4), custom_call_target="InvertDiagBlocksLowerTriangular" | custom-call | tf_op jit(solution)/shard_map/triangular_solve/custom-call.0 | solution.py:344
  124.7 0.0 copy-done
  124.7 1.1 fusion.1
  125.8 9.5 %fusion.14.x_ref = f32[128,4096]{1,0:T(8,128)} fusion(bf16[2048,128]{0,1:T(8,128)(2,1)S(1)} %fusion.1, bf16[2048,4096]{1,0:T(8,128)(2,1)} %bitcast.57), kind=kOutput, calls=%fused_computation.36 | convolution fusion | flops 2147483648 | bytes 19398656 | tf_op jit(solution)/shard_map/dot_general | solution.py:357
  135.3 41.8 %wide_sum.2 = bf16[128,4096]{1,0:T(8,128)(2,1)} custom-call(f32[128,4096]{1,0:T(8,128)} %fusion.14.x_ref), custom_call_target="tpu_custom_call" | custom-call | tf_op jit(solution)/shard_map/wide_sum/pallas_call | solution.py:324
  177.1 8.7 %fusion.15 = f32[2048,128]{1,0:T(8,128)S(1)} fusion(bf16[2048,4096]{1,0:T(8,128)(2,1)} %bitcast.58, bf16[128,4096]{1,0:T(8,128)(2,1)} %wide_sum.2), kind=kOutput, calls=%fused_computation.37 | convolution fusion | flops 2147483648 | bytes 18874368 | tf_op jit(solution)/shard_map/dot_general | solution.py:359
  185.8 2.5 fusion.16.x_ref
  188.2 14.0 %gram_sum.3 = f32[128,128]{1,0:T(8,128)} custom-call(f32[128,128]{1,0:T(8,128)} %fusion.16.x_ref), custom_call_target="tpu_custom_call" | custom-call | tf_op jit(solution)/shard_map/gram_sum/pallas_call | solution.py:191
  202.3 0.9 copy.13
  203.2 0.9 fusion.7
  204.1 11.7 %cholesky.55 = f32[128,128]{1,0:T(8,128)S(1)} custom-call(f32[128,128]{1,0:T(8,128)S(1)} %fusion.7), custom_call_target="Cholesky" | custom-call | tf_op jit(solution)/shard_map/jit(cholesky)/cholesky | solution.py:343
  215.8 0.6 compare_reduce_fusion
  216.4 0.7 fusion.5
  217.1 9.8 %custom-call.7 = f32[1,128,128]{1,2,0:T(8,128)S(1)} custom-call(f32[1,128,128]{2,1,0:T(8,128)S(1)} %fusion.5), custom_call_target="InvertDiagBlocksLowerTriangular" | custom-call | tf_op jit(solution)/shard_map/triangular_solve/custom-call.0 | solution.py:344
  226.9 1.1 fusion
  228.0 9.4 %fusion.2.x_ref = f32[128,4096]{1,0:T(8,128)} fusion(bf16[2048,4096]{1,0:T(8,128)(2,1)} %bitcast.59, f32[2048,128]{0,1:T(8,128)S(1)} %fusion), kind=kOutput, calls=%fused_computation.9 | convolution fusion | flops 2147745792 | bytes 19922944 | tf_op jit(solution)/shard_map/dot_general | solution.py:362
  237.4 1.3 copy.14
  238.7 46.3 %wide_sum.3 = f32[128,4096]{1,0:T(8,128)} custom-call(f32[128,4096]{1,0:T(8,128)} %fusion.2.x_ref), custom_call_target="tpu_custom_call" | custom-call | tf_op jit(solution)/shard_map/wide_sum/pallas_call | solution.py:324
  285.0 3.1 %broadcast_multiply_fusion = f32[128,4096]{1,0:T(8,128)} fusion(f32[128,4096]{1,0:T(8,128)} %wide_sum.3), kind=kLoop, calls=%fused_computation.4 | loop fusion | flops 524288 | bytes 4194304 | tf_op jit(solution)/shard_map/mul | solution.py:363
  (2 shorter events, 0.1 us)
Async XLA Ops:
  1.6 30.6 %collective-permute-start.5 = (bf16[1,4096]{1,0:T(2,128)(2,1)S(1)}, bf16[1,4096]{1,0:T(2,128)(2,1)S(1)}, u32[]{:S(2)}, u32[]{:S(2)}) collective-permute-start(bf16[1,4096]{1,0:T(2,128)(2,1)S(1)} %get-tuple-element.10), channel_id=1, source_target_pairs={{1,8},{2,9},{3,10},{4,11},{5,12},{6,13},{7,14},{9,16},{10,17},{11,... | collective-permute-start | bytes 24584 | tf_op jit(solution)/shard_map/ppermute | solution.py:87
  2.3 21.8 %collective-permute-start.4 = (bf16[1,4096]{1,0:T(2,128)(2,1)S(1)}, bf16[1,4096]{1,0:T(2,128)(2,1)S(1)}, u32[]{:S(2)}, u32[]{:S(2)}) collective-permute-start(bf16[1,4096]{1,0:T(2,128)(2,1)S(1)} %get-tuple-element.11), channel_id=1, source_target_pairs={{8,1},{9,2},{10,3},{11,4},{12,5},{13,6},{14,7},{16,9},{17,10},{18,... | collective-permute-start | bytes 24584 | tf_op jit(solution)/shard_map/ppermute | solution.py:87
  3.0 22.4 %collective-permute-start.2 = (bf16[1,4096]{1,0:T(2,128)(2,1)S(1)}, bf16[1,4096]{1,0:T(2,128)(2,1)S(1)}, u32[]{:S(2)}, u32[]{:S(2)}) collective-permute-start(bf16[1,4096]{1,0:T(2,128)(2,1)S(1)} %get-tuple-element.12), channel_id=1, source_target_pairs={{0,9},{1,10},{2,11},{3,12},{4,13},{5,14},{6,15},{8,17},{9,18},{10,... | collective-permute-start | bytes 24584 | tf_op jit(solution)/shard_map/ppermute | solution.py:87
  17.1 6.2 %copy-start.3 = (f32[3,3,4096]{2,1,0:T(4,128)S(1)}, f32[3,3,4096]{2,1,0:T(4,128)}, u32[]{:S(2)}) copy-start(f32[3,3,4096]{2,1,0:T(4,128)} %param.7) | copy-start | bytes 442372
  17.7 9.0 %collective-permute-start.3 = (bf16[64,4096]{1,0:T(8,128)(2,1)S(1)}, bf16[64,4096]{1,0:T(8,128)(2,1)S(1)}, u32[]{:S(2)}, u32[]{:S(2)}) collective-permute-start(bf16[64,4096]{1,0:T(8,128)(2,1)S(1)} %bitcast.62), channel_id=1, source_target_pairs={{0,1},{1,2},{2,3},{3,4},{4,5},{5,6},{6,7},{8,9},{9,10},{10,11},{11... | collective-permute-start | bytes 1572872 | tf_op jit(solution)/shard_map/ppermute | solution.py:87
  20.9 11.3 %collective-permute-start.6 = (bf16[64,4096]{1,0:T(8,128)(2,1)S(1)}, bf16[64,4096]{1,0:T(8,128)(2,1)S(1)}, u32[]{:S(2)}, u32[]{:S(2)}) collective-permute-start(bf16[64,4096]{1,0:T(8,128)(2,1)S(1)} %bitcast.61), channel_id=1, source_target_pairs={{1,0},{2,1},{3,2},{4,3},{5,4},{6,5},{7,6},{9,8},{10,9},{11,10},{12... | collective-permute-start | bytes 1572872 | tf_op jit(solution)/shard_map/ppermute | solution.py:87
  24.1 8.2 %collective-permute-start.7 = (bf16[1,4096]{1,0:T(2,128)(2,1)S(1)}, bf16[1,4096]{1,0:T(2,128)(2,1)S(1)}, u32[]{:S(2)}, u32[]{:S(2)}) collective-permute-start(bf16[1,4096]{1,0:T(2,128)(2,1)S(1)} %get-tuple-element.13), channel_id=1, source_target_pairs={{9,0},{10,1},{11,2},{12,3},{13,4},{14,5},{15,6},{17,8},{18,9},{19,... | collective-permute-start | bytes 24584 | tf_op jit(solution)/shard_map/ppermute | solution.py:87
  25.4 9.4 %collective-permute-start.1 = (bf16[32,4096]{1,0:T(8,128)(2,1)S(1)}, bf16[32,4096]{1,0:T(8,128)(2,1)S(1)}, u32[]{:S(2)}, u32[]{:S(2)}) collective-permute-start(bf16[32,4096]{1,0:T(8,128)(2,1)S(1)} %get-tuple-element.16), channel_id=1, source_target_pairs={{8,0},{9,1},{10,2},{11,3},{12,4},{13,5},{14,6},{15,7},{16,8},{17,9... | collective-permute-start | bytes 786440 | tf_op jit(solution)/shard_map/ppermute | solution.py:87
  26.7 9.5 %collective-permute-start = (bf16[32,4096]{1,0:T(8,128)(2,1)S(1)}, bf16[32,4096]{1,0:T(8,128)(2,1)S(1)}, u32[]{:S(2)}, u32[]{:S(2)}) collective-permute-start(bf16[32,4096]{1,0:T(8,128)(2,1)S(1)} %get-tuple-element.17), channel_id=1, source_target_pairs={{0,8},{1,9},{2,10},{3,11},{4,12},{5,13},{6,14},{7,15},{8,16},{9,17... | collective-permute-start | bytes 786440 | tf_op jit(solution)/shard_map/ppermute | solution.py:87
  34.8 1.5 copy-start.1
  36.2 0.7 copy-start.2
  75.5 49.2 %copy-start = (f32[2048,128]{1,0:T(8,128)S(1)}, f32[2048,128]{1,0:T(8,128)}, u32[]{:S(2)}) copy-start(f32[2048,128]{1,0:T(8,128)} %get-tuple-element.7) | copy-start | bytes 3145732

commit v2 on v1

--- a/solution.py
+++ b/solution.py
@@ -31,16 +31,87 @@
     pl.semaphore_wait(barrier, len(partners))
 
 
-def shifted_pairs(rows, cols, n_gy, n_gx):
-    pairs = []
-    for y in range(n_gy):
-        for x in range(n_gx):
-            if 0 <= y + rows < n_gy and 0 <= x + cols < n_gx:
-                pairs.append((y * n_gx + x, (y + rows) * n_gx + x + cols))
-    return pairs
-
-
-def smooth_kernel(x_ref, up_ref, down_ref, left_ref, right_ref, k_ref, t_ref, o_ref, s_ref, l_s, r_s):
+DIRECTIONS = ((1, 0), (-1, 0), (0, 1), (0, -1), (1, 1), (1, -1), (-1, 1), (-1, -1))
+
+
+def halo_kernel(n_gy, n_gx, x_ref, first_ref, last_ref, corner_ref, *rest):
+    outs, (send, recv) = rest[:8], rest[8:]
+    height = x_ref.shape[0]
+    y, x = lax.axis_index("gy"), lax.axis_index("gx")
+    sources = [x_ref.at[height - 1], x_ref.at[0], last_ref, first_ref] + [
+        corner_ref.at[i] for i in range(4)
+    ]
+    barrier = pltpu.get_barrier_semaphore()
+
+    def inside(rows, cols):
+        return (y + rows >= 0) & (y + rows < n_gy) & (x + cols >= 0) & (x + cols < n_gx)
+
+    present = 0
+    for rows, cols in DIRECTIONS:
+        there = inside(rows, cols)
+        present = present + jnp.where(there, 1, 0)
+
+        @pl.when(there)
+        def _():
+            pl.semaphore_signal(
+                barrier, inc=1, device_id=(y + rows, x + cols), device_id_type=MESH
+            )
+
+    pl.semaphore_wait(barrier, present)
+
+    def copy(i):
+        rows, cols = DIRECTIONS[i]
+        return pltpu.make_async_remote_copy(
+            sources[i], outs[i], send.at[i], recv.at[i], (y + rows, x + cols), MESH
+        )
+
+    for i, (rows, cols) in enumerate(DIRECTIONS):
+
+        @pl.when(inside(rows, cols))
+        def _():
+            copy(i).start()
+
+    for i, (rows, cols) in enumerate(DIRECTIONS):
+        arrives = inside(-rows, -cols)
+
+        @pl.when(arrives)
+        def _():
+            copy(i).wait_recv()
+
+        @pl.when(jnp.logical_not(arrives))
+        def _():
+            outs[i][...] = jnp.zeros_like(outs[i])
+
+    for i, (rows, cols) in enumerate(DIRECTIONS):
+
+        @pl.when(inside(rows, cols))
+        def _():
+            copy(i).wait_send()
+
+
+def halos(radiance, collective_id):
+    height, width, channels = radiance.shape
+    n_gy, n_gx = lax.axis_size("gy"), lax.axis_size("gx")
+    first, last = radiance[:, 0], radiance[:, width - 1]
+    corners = jnp.stack([last[height - 1], first[height - 1], last[0], first[0]])
+    corners = corners.reshape(4, 16, channels // 16)
+    shapes = [(width, channels)] * 2 + [(height, channels)] * 2 + [(16, channels // 16)] * 4
+    vmem = pl.BlockSpec(memory_space=pltpu.VMEM)
+    outs = pl.pallas_call(
+        functools.partial(halo_kernel, n_gy, n_gx),
+        out_shape=[jax.ShapeDtypeStruct(shape, radiance.dtype) for shape in shapes],
+        in_specs=[pl.BlockSpec(memory_space=pl.ANY), vmem, vmem, vmem],
+        out_specs=[vmem] * 8,
+        scratch_shapes=[pltpu.SemaphoreType.DMA((8,)), pltpu.SemaphoreType.DMA((8,))],
+        compiler_params=pltpu.CompilerParams(collective_id=collective_id, has_side_effects=True),
+        name="halo",
+    )(radiance, first, last, corners)
+    return outs[:4], jnp.stack(outs[4:]).reshape(4, channels)
+
+
+def smooth_kernel(
+    x_ref, up_ref, down_ref, left_ref, right_ref, c_ref, k_ref, t_ref, o_ref, s_ref, side, l_s, r_s
+):
     height, width, block = x_ref.shape
 
     @pl.when(pl.program_id(0) == 0)
@@ -49,11 +120,13 @@
 
     for part in range(block // LANES):
         lanes = pl.ds(part * LANES, LANES)
-        left = left_ref[:, lanes].astype(jnp.float32)
-        right = right_ref[:, lanes].astype(jnp.float32)
         k = [[k_ref[pl.ds(3 * a + b, 1), lanes] for b in range(3)] for a in range(3)]
-        l_s[...] = sum(k[a][0] * left[a : a + height] for a in range(3))
-        r_s[...] = sum(k[a][2] * right[a : a + height] for a in range(3))
+        corners = c_ref[:, lanes].astype(jnp.float32)
+        for b, middle, corner, sums in ((0, left_ref, 0, l_s), (2, right_ref, 1, r_s)):
+            side[pl.ds(8, height), :] = middle[:, lanes].astype(jnp.float32)
+            side[pl.ds(7, 1), :] = corners[corner : corner + 1]
+            side[pl.ds(8 + height, 1), :] = corners[corner + 2 : corner + 3]
+            sums[...] = sum(k[a][b] * side[pl.ds(7 + a, height), :] for a in range(3))
         place = lax.broadcasted_iota(jnp.int32, (width, LANES), 0)
 
         def row_out(h, above, here, below):
@@ -80,20 +153,8 @@
 def smooth_and_sketch(radiance, kernel, test_matrix):
     height, width, channels = radiance.shape
     k_width = test_matrix.shape[1]
-    n_gy, n_gx = lax.axis_size("gy"), lax.axis_size("gx")
     block = 512
-
-    def moved(value, rows, cols):
-        return lax.ppermute(value, ("gy", "gx"), shifted_pairs(rows, cols, n_gy, n_gx))
-
-    up = moved(radiance[height - 1], 1, 0)
-    down = moved(radiance[0], -1, 0)
-    sides = []
-    for cols, place in ((1, width - 1), (-1, 0)):
-        middle = moved(radiance[:, place], 0, cols)
-        top = moved(radiance[height - 1 :, place], 1, cols)
-        bottom = moved(radiance[:1, place], -1, cols)
-        sides.append(jnp.concatenate([top, middle, bottom], axis=0))
+    (up, down, left, right), corners = halos(radiance, 4)
     pixels = height * width
     return pl.pallas_call(
         smooth_kernel,
@@ -102,8 +163,9 @@
             pl.BlockSpec((height, width, block), lambda i: (0, 0, i)),
             pl.BlockSpec((width, block), lambda i: (0, i)),
             pl.BlockSpec((width, block), lambda i: (0, i)),
-            pl.BlockSpec((height + 2, block), lambda i: (0, i)),
-            pl.BlockSpec((height + 2, block), lambda i: (0, i)),
+            pl.BlockSpec((height, block), lambda i: (0, i)),
+            pl.BlockSpec((height, block), lambda i: (0, i)),
+            pl.BlockSpec((4, block), lambda i: (0, i)),
             pl.BlockSpec((9, block), lambda i: (0, i)),
             pl.BlockSpec((block, k_width), lambda i: (i, 0)),
         ],
@@ -116,6 +178,7 @@
             jax.ShapeDtypeStruct((pixels, k_width), jnp.float32),
         ],
         scratch_shapes=[
+            pltpu.VMEM((height + 16, LANES), jnp.float32),
             pltpu.VMEM((height, LANES), jnp.float32),
             pltpu.VMEM((height, LANES), jnp.float32),
         ],
@@ -126,7 +189,7 @@
             transcendentals=0,
         ),
         name="smooth_sketch",
-    )(radiance, up, down, sides[0], sides[1], kernel.reshape(9, channels), test_matrix)
+    )(radiance, up, down, left, right, corners, kernel.reshape(9, channels), test_matrix)
 
 
 def tree_sum(values):
@@ -336,13 +399,65 @@
     )(values)
 
 
+def inverse_factor_kernel(gram_ref, o_ref, state):
+    size = gram_ref.shape[0]
+    row = lax.broadcasted_iota(jnp.int32, (size, size), 0)
+    col = lax.broadcasted_iota(jnp.int32, (size, size), 1)
+    state[:, :size] = gram_ref[...]
+    state[:, size:] = jnp.where(row == col, 1.0, 0.0)
+    shape = (8, size)
+    place = lax.broadcasted_iota(jnp.int32, shape, 0)
+    for start in range(0, size, 8):
+        left = state[start : start + 8, :size]
+        right = state[start : start + 8, size:]
+        columns = [
+            jnp.broadcast_to(left[:, start + j : start + j + 1], shape) for j in range(8)
+        ]
+        scale = jnp.zeros(shape, jnp.float32)
+        for j in range(8):
+
+            def pivot_row(value):
+                return jnp.broadcast_to(value[j : j + 1], shape)
+
+            inverse = 1.0 / pivot_row(columns[j])
+            scale = jnp.where(place == j, inverse, scale)
+            if j == 7:
+                break
+            factor = jnp.where(place > j, columns[j] * inverse, 0.0)
+            left = left - factor * pivot_row(left)
+            right = right - factor * pivot_row(right)
+            for i in range(j + 1, 8):
+                columns[i] = columns[i] - factor * pivot_row(columns[i])
+        o_ref[start : start + 8, :] = right * jnp.sqrt(scale)
+        if start + 8 < size:
+            update = jnp.dot(
+                (left * scale).T,
+                jnp.concatenate([left, right], axis=1),
+                precision=lax.Precision.HIGHEST,
+                preferred_element_type=jnp.float32,
+            )
+            state[start + 8 :, :] = state[start + 8 :, :] - update[start + 8 :, :]
+
+
+def inverse_factor(gram):
+    size = gram.shape[0]
+    return pl.pallas_call(
+        inverse_factor_kernel,
+        out_shape=jax.ShapeDtypeStruct(gram.shape, jnp.float32),
+        in_specs=[pl.BlockSpec(memory_space=pltpu.VMEM)],
+        out_specs=pl.BlockSpec(memory_space=pltpu.VMEM),
+        scratch_shapes=[pltpu.VMEM((size, 2 * size), jnp.float32)],
+        name="inverse_factor",
+    )(gram)
+
+
 def factor_basis(values, collective_id):
     local_gram = jnp.dot(
         values.T, values, precision=lax.Precision.HIGHEST, preferred_element_type=jnp.float32
     )
-    triangle = jnp.linalg.cholesky(summed_gram(local_gram, collective_id))
-    return lax.linalg.triangular_solve(
-        triangle, values, left_side=False, lower=True, transpose_a=True
+    inverse = inverse_factor(summed_gram(local_gram, collective_id))
+    return jnp.dot(
+        values, inverse.T, precision=lax.Precision.HIGHEST, preferred_element_type=jnp.float32
     )
 
 

time: 289 us -> 251 us (0.87)
  other arithmetic: 52.5 us -> 4.41 us
  Pallas kernels: 161 us -> 194 us
  starting transfers between devices: 21.9 us -> 0 us
  waiting for transfers between devices: 2.97 us -> 0 us
    another operation x10 -> x2, other arithmetic: 45.7 us -> 1.31 us  [the longest x1 0.7 us: halos(): return (outs[:4], jnp.stack(outs[4:]).reshape(4, channels))]
    pallas_call x0 -> x3, Pallas kernels: none -> 34.7 us  [the longest x2 19.9 us: inverse_factor(): pl.pallas_call(inverse_factor_kernel, out_shape=jax.ShapeDtypeStruct(gram...]
    ppermute x8 -> x0, starting transfers between devices: 21.9 us -> none  [moved(): lax.ppermute(value, ('gy', 'gx'), shifted_pairs(rows, cols, n_gy, n_gx))]
    dot_general x0 -> x2, matrix products: none -> 4.03 us  [factor_basis(): jnp.dot(values, inverse.T, precision=lax.Precision.HIGHEST, preferred_ele...]
    ppermute x8 -> x0, waiting for transfers between devices: 2.97 us -> none  [moved(): lax.ppermute(value, ('gy', 'gx'), shifted_pairs(rows, cols, n_gy, n_gx))]
  transfers between devices with their start and end apart: 8 -> 0, of which waited for: 2 -> 0; matrix products, arithmetic and copies ran while one was open for 3% -> 0% of each run, Pallas kernels for 0% -> 0%
where the time goes in v2:
time: 251 us; the launch traced here: 250 us
  Pallas kernels  194 us (77%)
  matrix products  38.4 us (15%)
  local copies, waits for them, and re-layouts  12.5 us (5%)
  other arithmetic  4.41 us (2%)
    pallas_call x2, Pallas kernels, summed_wide(): pl.pallas_call(functools.partial(wide_kernel, orders), out_shape=jax.Shap...  87.4 us
    pallas_call x1, Pallas kernels, smooth_and_sketch(): pl.pallas_call(smooth_kernel, grid=(channels // block,), in_specs=[pl.Blo...  38.4 us
    pallas_call x2, Pallas kernels, summed_gram(): pl.pallas_call(functools.partial(gram_kernel, n_gy, n_gx), out_shape=jax....  33.9 us
    pallas_call x2, Pallas kernels, inverse_factor(): pl.pallas_call(inverse_factor_kernel, out_shape=jax.ShapeDtypeStruct(gram...  19.9 us
    pallas_call x1, Pallas kernels, halos(): pl.pallas_call(functools.partial(halo_kernel, n_gy, n_gx), out_shape=[jax...  14.8 us
    dot_general x1, matrix products, on_device(): jnp.dot(basis_half.T, flattened, preferred_element_type=jnp.float32)  9.84 us
    dot_general x1, matrix products, on_device(): jnp.dot(first_basis.T, flattened, preferred_element_type=jnp.float32)  9.48 us
    dot_general x1, matrix products, on_device(): second = jnp.dot(flattened, range_map.T, preferred_element_type=jnp.float32)  8.65 us

profile of v2, /device:TPU:0, one launch (start us, length us, event | category | flops | bytes accessed | tf_op | source)
XLA Modules:
  0.0 250.5 jit_solution(13784695282900847777)
XLA Ops:
  0.6 1.1 slice_reduce_fusion.3
  1.8 0.6 pad_maximum_fusion.corner_ref
  2.4 1.7 reshape.35.k_ref
  4.1 4.7 %fusion.2 = (bf16[64,1,4096]{2,1,0:T(2,128)(2,1)S(1)}, bf16[64,1,4096]{2,1,0:T(2,128)(2,1)S(1)}) fusion(bf16[64,32,4096]{2,1,0:T(8,128)(2,1)} %x_ref.3), kind=kLoop, calls=%fused_computation.13 | loop fusion | bytes 2097152 | tf_op jit(solution)/shard_map/slice | solution.py:95
  8.8 2.1 copy_bitcast_fusion
  10.9 14.8 %halo.1 = (bf16[32,4096]{1,0:T(8,128)(2,1)}, bf16[32,4096]{1,0:T(8,128)(2,1)}, bf16[64,4096]{1,0:T(8,128)(2,1)}, bf16[64,4096]{1,0:T(8,128)(2,1)}, bf16[16,256]{...) custom-call(bf16[64,32,4096]{2,1,0:T(8,128)(2,1)} %x_ref.3, ...), custom_call_target="tpu_custom_call" | custom-call | tf_op jit(solution)/shard_map/halo/pallas_call | solution.py:100
  25.7 0.7 copy.9
  26.4 0.7 copy.10
  27.1 0.7 copy.11
  27.9 0.7 copy.12
  28.6 0.7 pad_maximum_fusion.1.c_ref
  29.3 38.4 %smooth_sketch.1 = (bf16[64,32,4096]{2,1,0:T(8,128)(2,1)}, f32[2048,128]{1,0:T(8,128)}) custom-call(bf16[64,32,4096]{2,1,0:T(8,128)(2,1)} %x_ref.3, bf16[32,4096]{1,0:T(8,128)(2,1)} %get-tuple-element.12.up_ref, bf16[32,4096]{1,0:T(8,128)(2,1)} %get-tuple-element.13.down_ref, bf16[64,4096]{1,0:T(8,128)(2,1)} %get-tuple-element.14.left_ref, ...), custom_call_target="tpu_custom_call" | custom-call | flops 2298478592 | bytes 33554432 | tf_op jit(solution)/shard_map/smooth_sketch/pallas_call | solution.py:159
  67.7 4.0 %fusion.3.x_ref = f32[128,128]{1,0:T(8,128)} fusion(f32[2048,128]{1,0:T(8,128)} %get-tuple-element.21), kind=kOutput, calls=%fused_computation.14 | convolution fusion | flops 402653184 | bytes 1114112 | tf_op jit(solution)/shard_map/dot_general | solution.py:455
  71.6 19.9 %gram_sum.2.gram_ref = f32[128,128]{1,0:T(8,128)} custom-call(f32[128,128]{1,0:T(8,128)} %fusion.3.x_ref), custom_call_target="tpu_custom_call" | custom-call | tf_op jit(solution)/shard_map/gram_sum/pallas_call | solution.py:254
  91.6 9.9 %inverse_factor.2 = f32[128,128]{1,0:T(8,128)} custom-call(f32[128,128]{1,0:T(8,128)} %gram_sum.2.gram_ref), custom_call_target="tpu_custom_call" | custom-call | tf_op jit(solution)/shard_map/inverse_factor/pallas_call | solution.py:444
  101.5 2.2 convolution_convert_fusion
  103.7 9.5 %fusion.4.x_ref = f32[128,4096]{1,0:T(8,128)} fusion(bf16[2048,128]{1,0:T(8,128)(2,1)S(1)} %convolution_convert_fusion, bf16[2048,4096]{1,0:T(8,128)(2,1)} %bitcast.31), kind=kOutput, calls=%fused_computation.15 | convolution fusion | flops 2147483648 | bytes 19398656 | tf_op jit(solution)/shard_map/dot_general | solution.py:472
  113.2 41.7 %wide_sum.2 = bf16[128,4096]{1,0:T(8,128)(2,1)} custom-call(f32[128,4096]{1,0:T(8,128)} %fusion.4.x_ref), custom_call_target="tpu_custom_call" | custom-call | tf_op jit(solution)/shard_map/wide_sum/pallas_call | solution.py:387
  154.9 8.6 %fusion.5 = f32[2048,128]{1,0:T(8,128)S(1)} fusion(bf16[2048,4096]{1,0:T(8,128)(2,1)} %bitcast.32, bf16[128,4096]{1,0:T(8,128)(2,1)} %wide_sum.2), kind=kOutput, calls=%fused_computation.16 | convolution fusion | flops 2147483648 | bytes 18874368 | tf_op jit(solution)/shard_map/dot_general | solution.py:474
  163.6 2.5 fusion.6.x_ref
  166.1 14.0 %gram_sum.3.gram_ref = f32[128,128]{1,0:T(8,128)} custom-call(f32[128,128]{1,0:T(8,128)} %fusion.6.x_ref), custom_call_target="tpu_custom_call" | custom-call | tf_op jit(solution)/shard_map/gram_sum/pallas_call | solution.py:254
  180.1 9.9 %inverse_factor.3 = f32[128,128]{1,0:T(8,128)} custom-call(f32[128,128]{1,0:T(8,128)} %gram_sum.3.gram_ref), custom_call_target="tpu_custom_call" | custom-call | tf_op jit(solution)/shard_map/inverse_factor/pallas_call | solution.py:444
  190.0 1.8 convolution_multiply_fusion
  191.9 0.0 copy-start
  191.9 9.8 %fusion.x_ref = f32[128,4096]{1,0:T(8,128)} fusion(bf16[2048,4096]{1,0:T(8,128)(2,1)} %bitcast.33, f32[2048,128]{1,0:T(8,128)S(1)} %convolution_multiply_fusion), kind=kOutput, calls=%fused_computation.5 | convolution fusion | flops 2147745792 | bytes 19922944 | tf_op jit(solution)/shard_map/dot_general | solution.py:477
  201.7 45.7 %wide_sum.3 = f32[128,4096]{1,0:T(8,128)} custom-call(f32[128,4096]{1,0:T(8,128)} %fusion.x_ref), custom_call_target="tpu_custom_call" | custom-call | tf_op jit(solution)/shard_map/wide_sum/pallas_call | solution.py:387
  247.4 3.1 %broadcast_multiply_fusion = f32[128,4096]{1,0:T(8,128)} fusion(f32[128,4096]{1,0:T(8,128)} %wide_sum.3), kind=kLoop, calls=%fused_computation.2 | loop fusion | flops 524288 | bytes 4194304 | tf_op jit(solution)/shard_map/mul | solution.py:478
  250.5 0.0 copy-done
  (4 shorter events, 0.0 us)
Async XLA Ops:
  191.9 58.6 %copy-start = (f32[2048,128]{1,0:T(8,128)}, f32[2048,128]{1,0:T(8,128)S(1)}, u32[]{:S(2)}) copy-start(f32[2048,128]{1,0:T(8,128)S(1)} %convolution_multiply_fusion) | copy-start | bytes 3145732

commit v3 on v2

--- a/solution.py
+++ b/solution.py
@@ -272,131 +272,204 @@
     )(gram)
 
 
-def wide_orders(n_gy, n_gx):
-    x_bits = [("gx", b) for b in range(n_gx.bit_length() - 1)]
-    y_bits = [("gy", b) for b in range(n_gy.bit_length() - 1)]
-    first, across = x_bits[:1], x_bits[1:]
-    return [first + across + y_bits, first + across[::-1] + y_bits]
-
-
-def halvings(rows, cols, count):
+def wide_orders(n_gy, n_gx, chunks):
+    x_steps = [("gx", b, 1) for b in range(n_gx.bit_length() - 1)]
+    y_bits = n_gy.bit_length() - 1
+    y_steps = [("gy", b, 1) for b in range(max(y_bits - 2, 0))]
+    if y_bits >= 2:
+        y_steps.append(("gy", y_bits - 2, 2))
+    elif y_bits:
+        y_steps.append(("gy", 0, 1))
+    first, across = x_steps[:1], x_steps[1:]
+    return [first + (across[::-1] if q % 2 else across) + y_steps for q in range(chunks)]
+
+
+def kept_shapes(rows, cols, order):
     shapes = []
-    for _ in range(count):
-        if rows > 16:
-            rows //= 2
+    for _, _, bits in order:
+        if rows >= 16 * 2**bits:
+            rows //= 2**bits
         else:
-            cols //= 2
+            cols //= 2**bits
         shapes.append((rows, cols))
     return shapes
 
 
-def wide_kernel(orders, x_ref, o_ref, *scratch):
+def wide_kernel(orders, blocks, again, b_ref, f_ref, *rest):
+    o_ref, work, held, load = rest[:4]
+    rest = rest[4:]
+    gathered = o_ref
+    if again:
+        gathered, rest = rest[0], rest[1:]
     steps, chunks = len(orders[0]), len(orders)
-    rows, cols = x_ref.shape
+    recv = [rest[q * steps : (q + 1) * steps] for q in range(chunks)]
+    s_send, s_recv, g_send, g_recv = rest[chunks * steps :]
+    rows, cols = work.shape
     wide = cols // chunks
-    work = scratch[0]
-    recv = [scratch[1 + q * steps : 1 + (q + 1) * steps] for q in range(chunks)]
-    s_send, s_recv, g_send, g_recv = scratch[1 + chunks * steps :]
+    block = cols // blocks
     me = {"gx": lax.axis_index("gx"), "gy": lax.axis_index("gy")}
 
-    def partner(axis, bit):
+    def partner(step, d):
+        axis, bit, bits = step
         other = dict(me)
-        other[axis] = flipped(me[axis], 1 << bit, bit + 1)
+        other[axis] = flipped(me[axis], d << bit, bit + bits)
         return (other["gy"], other["gx"])
 
-    greet([partner(*which) for which in orders[0]])
-    shapes = halvings(rows, wide, steps)
-    kept, sent = [], []
+    loads = [
+        pltpu.make_async_copy(f_ref.at[:, pl.ds(i * block, block)], held.at[i], load.at[i])
+        for i in range(blocks)
+    ]
+    for copy in loads:
+        copy.start()
+    barrier = pltpu.get_barrier_semaphore()
+    others = [partner(step, d) for step in orders[0] for d in range(1, 2 ** step[2])]
+    for other in others:
+        pl.semaphore_signal(barrier, inc=1, device_id=other, device_id_type=MESH)
+
+    places, shapes, index, count = [], [], [], 0
     for q in range(chunks):
-        row, col = 0, q * wide
-        size = (rows, wide)
-        kept_q, sent_q = [], []
-        for s, (axis, bit) in enumerate(orders[q]):
-            mine = bit_of(me[axis], bit)
-            h, w = shapes[s]
-            if h < size[0]:
-                kept_q.append((row + mine * h, col))
-                sent_q.append((row + (1 - mine) * h, col))
-            else:
-                kept_q.append((row, col + mine * w))
-                sent_q.append((row, col + (1 - mine) * w))
-            row, col = kept_q[-1]
+        row, col, size = 0, q * wide, (rows, wide)
+        shapes.append(kept_shapes(rows, wide, orders[q]))
+        places.append([])
+        index.append([])
+        for s, (axis, bit, bits) in enumerate(orders[q]):
+            h, w = shapes[q][s]
+            at = []
+            for d in range(2**bits):
+                part = flipped((me[axis] // 2**bit) % 2**bits, d, bits)
+                at.append((row + part * h, col) if h < size[0] else (row, col + part * w))
+            places[q].append(at)
+            index[q].append(count - 1)
+            count += 2**bits - 1
+            row, col = at[0]
             size = (h, w)
-        kept.append(kept_q)
-        sent.append(sent_q)
-
-    def region(place, shape):
-        row = place[0] if isinstance(place[0], int) else pl.multiple_of(place[0], 16)
-        col = place[1] if isinstance(place[1], int) else pl.multiple_of(place[1], LANES)
+
+    def region(q, s, d):
+        (row, col), shape = places[q][s][d], shapes[q][s]
+        row = row if isinstance(row, int) else pl.multiple_of(row, 16)
+        col = col if isinstance(col, int) else pl.multiple_of(col, LANES)
         return (pl.ds(row, shape[0]), pl.ds(col, shape[1]))
 
-    def reduce_copy(q, s):
-        source = x_ref if s == 0 else work
-        return pltpu.make_async_remote_copy(
-            source.at[region(sent[q][s], shapes[s])],
-            recv[q][s],
-            s_send.at[q * steps + s],
-            s_recv.at[q * steps + s],
-            partner(*orders[q][s]),
-            MESH,
-        )
-
-    def gather_copy(q, s, outgoing):
-        place = region(kept[q][s] if outgoing else sent[q][s], shapes[s])
-        return pltpu.make_async_remote_copy(
-            o_ref.at[place],
-            o_ref.at[place],
-            g_send.at[q * steps + s],
-            g_recv.at[q * steps + s],
-            partner(*orders[q][s]),
-            MESH,
-        )
-
-    for q in range(chunks):
-        reduce_copy(q, 0).start()
-    for s in range(steps):
-        for q in range(chunks):
-            reduce_copy(q, s).wait_recv()
-            here = region(kept[q][s], shapes[s])
-            source = x_ref if s == 0 else work
-            total = source[here] + recv[q][s][...]
+    def reduce_copies(q, s):
+        copies = []
+        for d in range(1, 2 ** orders[q][s][2]):
+            sem = index[q][s] + d
+            copies.append(
+                pltpu.make_async_remote_copy(
+                    work.at[region(q, s, d)],
+                    recv[q][s].at[d - 1],
+                    s_send.at[sem],
+                    s_recv.at[sem],
+                    partner(orders[q][s], d),
+                    MESH,
+                )
+            )
+        return copies
+
+    def gather_copies(q, s, outgoing):
+        copies = []
+        for d in range(1, 2 ** orders[q][s][2]):
+            sem = index[q][s] + d
+            at = gathered.at[region(q, s, 0 if outgoing else d)]
+            copies.append(
+                pltpu.make_async_remote_copy(
+                    at, at, g_send.at[sem], g_recv.at[sem], partner(orders[q][s], d), MESH
+                )
+            )
+        return copies
+
+    def start(copies):
+        for copy in copies:
+            copy.start()
+
+    def advance(q, stage):
+        if stage < steps:
+            s = stage
+            for copy in reduce_copies(q, s):
+                copy.wait_recv()
+            here = region(q, s, 0)
+            parts = [work[here]] + [recv[q][s][d - 1] for d in range(1, 2 ** orders[q][s][2])]
+            total = tree_sum(parts)
             if s + 1 < steps:
                 work[here] = total
-                reduce_copy(q, s + 1).start()
+                start(reduce_copies(q, s + 1))
             else:
-                o_ref[here] = total.astype(o_ref.dtype)
-                gather_copy(q, s, True).start()
-    for s in reversed(range(steps)):
+                gathered[here] = total.astype(gathered.dtype)
+                start(gather_copies(q, s, True))
+            return
+        s = 2 * steps - 1 - stage
+        for copy in gather_copies(q, s, False):
+            copy.wait_recv()
+        if s > 0:
+            start(gather_copies(q, s - 1, True))
+        elif again:
+            per = wide // block
+            for i in range(q * per, (q + 1) * per):
+                part = lax.dot_general(
+                    held[i],
+                    gathered[:, i * block : (i + 1) * block],
+                    (((1,), (1,)), ((), ())),
+                    preferred_element_type=jnp.float32,
+                )
+                o_ref[...] = part if i == 0 else o_ref[...] + part
+
+    stages = [0] * chunks
+    for q in range(chunks):
+        per = wide // block
+        for i in range(q * per, (q + 1) * per):
+            loads[i].wait()
+            work[:, i * block : (i + 1) * block] = jnp.dot(
+                b_ref[...], held[i], preferred_element_type=jnp.float32
+            )
+        if q == 0:
+            pl.semaphore_wait(barrier, len(others))
+        start(reduce_copies(q, 0))
+        for p in range(q):
+            advance(p, stages[p])
+            stages[p] += 1
+    while min(stages) < 2 * steps:
         for q in range(chunks):
-            gather_copy(q, s, False).wait_recv()
-            if s > 0:
-                gather_copy(q, s - 1, True).start()
-    for s in range(steps):
-        for q in range(chunks):
-            reduce_copy(q, s).wait_send()
-            gather_copy(q, s, True).wait_send()
-
-
-def summed_wide(values, dtype, collective_id):
+            if stages[q] < 2 * steps:
+                advance(q, stages[q])
+                stages[q] += 1
+    for q in range(chunks):
+        for s in range(steps):
+            for copy in reduce_copies(q, s) + gather_copies(q, s, True):
+                copy.wait_send()
+
+
+def wide_product(basis, flattened, collective_id, again):
     n_gy, n_gx = lax.axis_size("gy"), lax.axis_size("gx")
-    orders = wide_orders(n_gy, n_gx)
-    rows, cols = values.shape
-    steps, chunks = len(orders[0]), len(orders)
-    shapes = halvings(rows, cols // chunks, steps)
-    dma = pltpu.SemaphoreType.DMA((chunks * steps,))
+    pixels, cols = flattened.shape
+    rows = basis.shape[1]
+    chunks = min(4, rows * cols // (16 * LANES * n_gy * n_gx))
+    blocks = 8
+    orders = wide_orders(n_gy, n_gx, chunks)
+    shapes = [kept_shapes(rows, cols // chunks, order) for order in orders]
+    copies = chunks * sum(2**bits - 1 for _, _, bits in orders[0])
+    dma = pltpu.SemaphoreType.DMA
+    scratch = [
+        pltpu.VMEM((rows, cols), jnp.float32),
+        pltpu.VMEM((blocks, pixels, cols // blocks), jnp.bfloat16),
+        dma((blocks,)),
+    ]
+    if again:
+        scratch.append(pltpu.VMEM((rows, cols), jnp.bfloat16))
+    for order, of_chunk in zip(orders, shapes):
+        for (_, _, bits), shape in zip(order, of_chunk):
+            scratch.append(pltpu.VMEM((2**bits - 1, *shape), jnp.float32))
+    vmem = pl.BlockSpec(memory_space=pltpu.VMEM)
     return pl.pallas_call(
-        functools.partial(wide_kernel, orders),
-        out_shape=jax.ShapeDtypeStruct(values.shape, dtype),
-        in_specs=[pl.BlockSpec(memory_space=pltpu.VMEM)],
-        out_specs=pl.BlockSpec(memory_space=pltpu.VMEM),
-        scratch_shapes=[pltpu.VMEM((rows, cols), jnp.float32)]
-        + [pltpu.VMEM(shape, jnp.float32) for _ in range(chunks) for shape in shapes]
-        + [dma] * 4,
+        functools.partial(wide_kernel, orders, blocks, again),
+        out_shape=jax.ShapeDtypeStruct((pixels, rows) if again else (rows, cols), jnp.float32),
+        in_specs=[vmem, pl.BlockSpec(memory_space=pl.ANY)],
+        out_specs=vmem,
+        scratch_shapes=scratch + [dma((copies,))] * 4,
         compiler_params=pltpu.CompilerParams(
             collective_id=collective_id, has_side_effects=True, vmem_limit_bytes=VMEM_LIMIT
         ),
-        name="wide_sum",
-    )(values)
+        name="wide_product",
+    )(basis.T, flattened)
 
 
 def inverse_factor_kernel(gram_ref, o_ref, state):
@@ -468,14 +541,11 @@
     smoothed, sketch = smooth_and_sketch(radiance, kernel, test_matrix)
     flattened = smoothed.reshape(height * breadth, channels)
     first_basis = factor_basis(sketch, 0).astype(jnp.bfloat16)
-    range_map = summed_wide(
-        jnp.dot(first_basis.T, flattened, preferred_element_type=jnp.float32), jnp.bfloat16, 2
-    )
-    second = jnp.dot(flattened, range_map.T, preferred_element_type=jnp.float32)
+    second = wide_product(first_basis, flattened, 2, True)
     basis_out = factor_basis(second, 1) * math.sqrt(pixel_count)
     basis_half = basis_out.astype(jnp.bfloat16)
-    projected = jnp.dot(basis_half.T, flattened, preferred_element_type=jnp.float32)
-    coeffs = summed_wide(projected, jnp.float32, 3) * (math.sqrt(channels) / pixel_count)
+    projected = wide_product(basis_half, flattened, 3, False)
+    coeffs = projected * (math.sqrt(channels) / pixel_count)
     return (basis_out.reshape(height, breadth, basis_out.shape[1]), coeffs)
 
 

time: 251 us -> 238 us (0.948)
  matrix products: 38.4 us -> 12.7 us
  Pallas kernels: 194 us -> 204 us
    dot_general x3 -> x0, matrix products: 28 us -> none  [the longest x1 9.84 us: on_device(): jnp.dot(basis_half.T, flattened, preferred_element_type=jnp.float32)]
    pallas_call x2, Pallas kernels: 87.4 us -> 97.2 us  [wide_product(): pl.pallas_call(functools.partial(wide_kernel, orders, blocks, again), out...]
where the time goes in v3:
time: 238 us; the launch traced here: 237 us
  Pallas kernels  204 us (86%)
  local copies, waits for them, and re-layouts  13.8 us (6%)
  matrix products  12.7 us (5%)
  other arithmetic  5.27 us (2%)
    pallas_call x2, Pallas kernels, wide_product(): pl.pallas_call(functools.partial(wide_kernel, orders, blocks, again), out...  97.2 us
    pallas_call x1, Pallas kernels, smooth_and_sketch(): pl.pallas_call(smooth_kernel, grid=(channels // block,), in_specs=[pl.Blo...  38.4 us
    pallas_call x2, Pallas kernels, summed_gram(): pl.pallas_call(functools.partial(gram_kernel, n_gy, n_gx), out_shape=jax....  34.2 us
    pallas_call x2, Pallas kernels, inverse_factor(): pl.pallas_call(inverse_factor_kernel, out_shape=jax.ShapeDtypeStruct(gram...  19.9 us
    pallas_call x1, Pallas kernels, halos(): pl.pallas_call(functools.partial(halo_kernel, n_gy, n_gx), out_shape=[jax...  14.8 us
    dot_general x2, matrix products, factor_basis(): jnp.dot(values.T, values, precision=lax.Precision.HIGHEST, preferred_elem...  8.17 us

profile of v3, /device:TPU:0, one launch (start us, length us, event | category | flops | bytes accessed | tf_op | source)
XLA Modules:
  0.0 237.0 jit_solution(7767288227412725466)
XLA Ops:
  0.6 1.1 slice_reduce_fusion.3
  1.8 0.6 pad_maximum_fusion.corner_ref
  2.4 1.7 reshape.35.k_ref
  4.1 4.7 %fusion = (bf16[64,1,4096]{2,1,0:T(2,128)(2,1)S(1)}, bf16[64,1,4096]{2,1,0:T(2,128)(2,1)S(1)}) fusion(bf16[64,32,4096]{2,1,0:T(8,128)(2,1)} %x_ref.3), kind=kLoop, calls=%fused_computation.12 | loop fusion | bytes 2097152 | tf_op jit(solution)/shard_map/slice | solution.py:95
  8.8 2.1 copy_bitcast_fusion
  10.9 14.8 %halo.1 = (bf16[32,4096]{1,0:T(8,128)(2,1)}, bf16[32,4096]{1,0:T(8,128)(2,1)}, bf16[64,4096]{1,0:T(8,128)(2,1)}, bf16[64,4096]{1,0:T(8,128)(2,1)}, bf16[16,256]{...) custom-call(bf16[64,32,4096]{2,1,0:T(8,128)(2,1)} %x_ref.3, ...), custom_call_target="tpu_custom_call" | custom-call | tf_op jit(solution)/shard_map/halo/pallas_call | solution.py:100
  25.7 0.7 copy.16
  26.4 0.7 copy.17
  27.1 0.7 copy.18
  27.9 0.7 copy.19
  28.6 0.7 pad_maximum_fusion.1.c_ref
  29.3 38.4 %smooth_sketch.1 = (bf16[64,32,4096]{2,1,0:T(8,128)(2,1)}, f32[2048,128]{1,0:T(8,128)}) custom-call(bf16[64,32,4096]{2,1,0:T(8,128)(2,1)} %x_ref.3, bf16[32,4096]{1,0:T(8,128)(2,1)} %get-tuple-element.12.up_ref, bf16[32,4096]{1,0:T(8,128)(2,1)} %get-tuple-element.13.down_ref, bf16[64,4096]{1,0:T(8,128)(2,1)} %get-tuple-element.14.left_ref, ...), custom_call_target="tpu_custom_call" | custom-call | flops 2298478592 | bytes 33554432 | tf_op jit(solution)/shard_map/smooth_sketch/pallas_call | solution.py:159
  67.7 0.0 copy-start.1
  67.7 4.1 %fusion.1.x_ref = f32[128,128]{1,0:T(8,128)} fusion(f32[2048,128]{1,0:T(8,128)} %get-tuple-element.20), kind=kOutput, calls=%fused_computation.13 | convolution fusion | flops 402653184 | bytes 1114112 | tf_op jit(solution)/shard_map/dot_general | solution.py:528
  71.8 19.9 %gram_sum.2.gram_ref = f32[128,128]{1,0:T(8,128)} custom-call(f32[128,128]{1,0:T(8,128)} %fusion.1.x_ref), custom_call_target="tpu_custom_call" | custom-call | tf_op jit(solution)/shard_map/gram_sum/pallas_call | solution.py:254
  91.7 9.9 %inverse_factor.2 = f32[128,128]{1,0:T(8,128)} custom-call(f32[128,128]{1,0:T(8,128)} %gram_sum.2.gram_ref), custom_call_target="tpu_custom_call" | custom-call | tf_op jit(solution)/shard_map/inverse_factor/pallas_call | solution.py:517
  101.6 0.0 copy-done.1
  101.6 2.7 %convolution_convert_fusion.b_ref = bf16[128,2048]{1,0:T(8,128)(2,1)} fusion(f32[128,128]{1,0:T(8,128)} %inverse_factor.2, f32[2048,128]{1,0:T(8,128)S(1)} %copy-done.1), kind=kOutput, calls=%fused_computation.1 | convolution fusion | flops 402915328 | bytes 1638400 | tf_op jit(solution)/shard_map/dot_general | solution.py:532
  104.3 48.4 %wide_product.2 = f32[2048,128]{1,0:T(8,128)} custom-call(bf16[128,2048]{1,0:T(8,128)(2,1)} %convolution_convert_fusion.b_ref, bf16[2048,4096]{1,0:T(8,128)(2,1)} %bitcast.28), custom_call_target="tpu_custom_call" | custom-call | tf_op jit(solution)/shard_map/wide_product/pallas_call | solution.py:462
  152.7 0.0 copy-start
  152.7 4.1 %fusion.2.x_ref = f32[128,128]{1,0:T(8,128)} fusion(f32[2048,128]{1,0:T(8,128)} %wide_product.2), kind=kOutput, calls=%fused_computation.14 | convolution fusion | flops 402653184 | bytes 1114112 | tf_op jit(solution)/shard_map/dot_general | solution.py:528
  156.8 14.3 %gram_sum.3.gram_ref = f32[128,128]{1,0:T(8,128)} custom-call(f32[128,128]{1,0:T(8,128)} %fusion.2.x_ref), custom_call_target="tpu_custom_call" | custom-call | tf_op jit(solution)/shard_map/gram_sum/pallas_call | solution.py:254
  171.1 9.9 %inverse_factor.3 = f32[128,128]{1,0:T(8,128)} custom-call(f32[128,128]{1,0:T(8,128)} %gram_sum.3.gram_ref), custom_call_target="tpu_custom_call" | custom-call | tf_op jit(solution)/shard_map/inverse_factor/pallas_call | solution.py:517
  181.0 0.0 copy-done
  181.0 1.9 convolution_multiply_fusion
  183.0 0.9 convert_bitcast_fusion.b_ref
  183.8 48.7 %wide_product.3 = f32[128,4096]{1,0:T(8,128)} custom-call(bf16[128,2048]{1,0:T(8,128)(2,1)} %convert_bitcast_fusion.b_ref, bf16[2048,4096]{1,0:T(8,128)(2,1)} %bitcast.29), custom_call_target="tpu_custom_call" | custom-call | tf_op jit(solution)/shard_map/wide_product/pallas_call | solution.py:462
  232.6 3.1 %broadcast_multiply_fusion = f32[128,4096]{1,0:T(8,128)} fusion(f32[128,4096]{1,0:T(8,128)} %wide_product.3), kind=kLoop, calls=%fused_computation.2 | loop fusion | flops 524288 | bytes 4194304 | tf_op jit(solution)/shard_map/mul | solution.py:548
  235.7 1.3 copy.12
  (4 shorter events, 0.0 us)
Async XLA Ops:
  67.7 33.9 %copy-start.1 = (f32[2048,128]{1,0:T(8,128)S(1)}, f32[2048,128]{1,0:T(8,128)}, u32[]{:S(2)}) copy-start(f32[2048,128]{1,0:T(8,128)} %get-tuple-element.20) | copy-start | bytes 3145732
  152.7 28.3 %copy-start = (f32[2048,128]{1,0:T(8,128)S(1)}, f32[2048,128]{1,0:T(8,128)}, u32[]{:S(2)}) copy-start(f32[2048,128]{1,0:T(8,128)} %wide_product.2) | copy-start | bytes 3145732

commit v4 on v3

--- a/solution.py
+++ b/solution.py
@@ -34,13 +34,11 @@
 DIRECTIONS = ((1, 0), (-1, 0), (0, 1), (0, -1), (1, 1), (1, -1), (-1, 1), (-1, -1))
 
 
-def halo_kernel(n_gy, n_gx, x_ref, first_ref, last_ref, corner_ref, *rest):
+def halo_kernel(n_gy, n_gx, x_ref, first_ref, last_ref, c0, c1, c2, c3, *rest):
     outs, (send, recv) = rest[:8], rest[8:]
     height = x_ref.shape[0]
     y, x = lax.axis_index("gy"), lax.axis_index("gx")
-    sources = [x_ref.at[height - 1], x_ref.at[0], last_ref, first_ref] + [
-        corner_ref.at[i] for i in range(4)
-    ]
+    sources = [x_ref.at[height - 1], x_ref.at[0], last_ref, first_ref, c0, c1, c2, c3]
     barrier = pltpu.get_barrier_semaphore()
 
     def inside(rows, cols):
@@ -93,26 +91,31 @@
     height, width, channels = radiance.shape
     n_gy, n_gx = lax.axis_size("gy"), lax.axis_size("gx")
     first, last = radiance[:, 0], radiance[:, width - 1]
-    corners = jnp.stack([last[height - 1], first[height - 1], last[0], first[0]])
-    corners = corners.reshape(4, 16, channels // 16)
-    shapes = [(width, channels)] * 2 + [(height, channels)] * 2 + [(16, channels // 16)] * 4
+    corners = [
+        radiance[row : row + 1, col].astype(jnp.float32)
+        for row in (height - 1, 0)
+        for col in (width - 1, 0)
+    ]
+    shapes = [(width, channels)] * 2 + [(height, channels)] * 2 + [(1, channels)] * 4
+    kinds = [radiance.dtype] * 4 + [jnp.float32] * 4
     vmem = pl.BlockSpec(memory_space=pltpu.VMEM)
     outs = pl.pallas_call(
         functools.partial(halo_kernel, n_gy, n_gx),
-        out_shape=[jax.ShapeDtypeStruct(shape, radiance.dtype) for shape in shapes],
-        in_specs=[pl.BlockSpec(memory_space=pl.ANY), vmem, vmem, vmem],
+        out_shape=[jax.ShapeDtypeStruct(*each) for each in zip(shapes, kinds)],
+        in_specs=[pl.BlockSpec(memory_space=pl.ANY)] + [vmem] * 6,
         out_specs=[vmem] * 8,
         scratch_shapes=[pltpu.SemaphoreType.DMA((8,)), pltpu.SemaphoreType.DMA((8,))],
         compiler_params=pltpu.CompilerParams(collective_id=collective_id, has_side_effects=True),
         name="halo",
-    )(radiance, first, last, corners)
-    return outs[:4], jnp.stack(outs[4:]).reshape(4, channels)
+    )(radiance, first, last, *corners)
+    return outs
 
 
 def smooth_kernel(
-    x_ref, up_ref, down_ref, left_ref, right_ref, c_ref, k_ref, t_ref, o_ref, s_ref, side, l_s, r_s
+    x_ref, up_ref, down_ref, left_ref, right_ref, c0, c1, c2, c3, k_ref, t_ref, o_ref, s_ref, flat
 ):
     height, width, block = x_ref.shape
+    pitch = width + 8
 
     @pl.when(pl.program_id(0) == 0)
     def _():
@@ -120,30 +123,44 @@
 
     for part in range(block // LANES):
         lanes = pl.ds(part * LANES, LANES)
-        k = [[k_ref[pl.ds(3 * a + b, 1), lanes] for b in range(3)] for a in range(3)]
-        corners = c_ref[:, lanes].astype(jnp.float32)
-        for b, middle, corner, sums in ((0, left_ref, 0, l_s), (2, right_ref, 1, r_s)):
-            side[pl.ds(8, height), :] = middle[:, lanes].astype(jnp.float32)
-            side[pl.ds(7, 1), :] = corners[corner : corner + 1]
-            side[pl.ds(8 + height, 1), :] = corners[corner + 2 : corner + 3]
-            sums[...] = sum(k[a][b] * side[pl.ds(7 + a, height), :] for a in range(3))
-        place = lax.broadcasted_iota(jnp.int32, (width, LANES), 0)
-
-        def row_out(h, above, here, below):
-            p = [k[0][b] * above + k[1][b] * here + k[2][b] * below for b in range(3)]
-            before = jnp.where(place == 0, l_s[pl.ds(h, 1), :], pltpu.roll(p[0], 1, 0))
-            after = jnp.where(place == width - 1, r_s[pl.ds(h, 1), :], pltpu.roll(p[2], width - 1, 0))
-            o_ref[h, :, lanes] = (p[1] + before + after).astype(jnp.bfloat16)
-
-        def step(h, carry):
-            above, here = carry
-            below = x_ref[h + 1, :, lanes].astype(jnp.float32)
-            row_out(h, above, here, below)
-            return here, below
-
-        first = (up_ref[:, lanes].astype(jnp.float32), x_ref[0, :, lanes].astype(jnp.float32))
-        above, here = lax.fori_loop(0, height - 1, step, first, unroll=3)
-        row_out(height - 1, above, here, down_ref[:, lanes].astype(jnp.float32))
+
+        def fill(h, carry):
+            flat[pl.ds(pl.multiple_of((h + 1) * pitch + 8, 8), width), :] = x_ref[h, :, lanes].astype(
+                jnp.float32
+            )
+            return carry
+
+        lax.fori_loop(0, height, fill, 0, unroll=8)
+        flat[pl.ds(8, width), :] = up_ref[:, lanes].astype(jnp.float32)
+        flat[pl.ds((height + 1) * pitch + 8, width), :] = down_ref[:, lanes].astype(jnp.float32)
+        flat[pl.ds(pitch + 7, height, stride=pitch), :] = left_ref[:, lanes].astype(jnp.float32)
+        flat[pl.ds(2 * pitch, height, stride=pitch), :] = right_ref[:, lanes].astype(jnp.float32)
+        flat[pl.ds(7, 1), :] = c0[:, lanes]
+        flat[pl.ds(pitch, 1), :] = c1[:, lanes]
+        flat[pl.ds((height + 1) * pitch + 7, 1), :] = c2[:, lanes]
+        flat[pl.ds((height + 2) * pitch, 1), :] = c3[:, lanes]
+        k = [
+            [jnp.broadcast_to(k_ref[a, pl.ds(b, 1), lanes], (16, LANES)) for b in range(3)]
+            for a in range(3)
+        ]
+        for first in range(0, width, 16):
+
+            def shifts(h):
+                start = pl.multiple_of(h * pitch, 8) + 7 + first
+                return [flat[pl.ds(start + b, 16), :] for b in range(3)]
+
+            def step(h, carry):
+                above, here = carry
+                below = shifts(h + 2)
+                total = [
+                    k[0][b] * above[b] + k[1][b] * here[b] + k[2][b] * below[b] for b in range(3)
+                ]
+                o_ref[h, pl.ds(first, 16), lanes] = (total[0] + total[1] + total[2]).astype(
+                    jnp.bfloat16
+                )
+                return here, below
+
+            lax.fori_loop(0, height, step, (shifts(0), shifts(1)), unroll=8)
 
     s_ref[...] += jnp.dot(
         o_ref[...].reshape(height * width, block), t_ref[...], preferred_element_type=jnp.float32
@@ -154,7 +171,7 @@
     height, width, channels = radiance.shape
     k_width = test_matrix.shape[1]
     block = 512
-    (up, down, left, right), corners = halos(radiance, 4)
+    border = halos(radiance, 4)
     pixels = height * width
     return pl.pallas_call(
         smooth_kernel,
@@ -165,8 +182,10 @@
             pl.BlockSpec((width, block), lambda i: (0, i)),
             pl.BlockSpec((height, block), lambda i: (0, i)),
             pl.BlockSpec((height, block), lambda i: (0, i)),
-            pl.BlockSpec((4, block), lambda i: (0, i)),
-            pl.BlockSpec((9, block), lambda i: (0, i)),
+        ]
+        + [pl.BlockSpec((1, block), lambda i: (0, i))] * 4
+        + [
+            pl.BlockSpec((3, 3, block), lambda i: (0, 0, i)),
             pl.BlockSpec((block, k_width), lambda i: (i, 0)),
         ],
         out_specs=[
@@ -178,9 +197,7 @@
             jax.ShapeDtypeStruct((pixels, k_width), jnp.float32),
         ],
         scratch_shapes=[
-            pltpu.VMEM((height + 16, LANES), jnp.float32),
-            pltpu.VMEM((height, LANES), jnp.float32),
-            pltpu.VMEM((height, LANES), jnp.float32),
+            pltpu.VMEM(((height + 3) * (width + 8), LANES), jnp.float32),
         ],
         compiler_params=pltpu.CompilerParams(vmem_limit_bytes=VMEM_LIMIT),
         cost_estimate=pl.CostEstimate(
@@ -189,7 +206,7 @@
             transcendentals=0,
         ),
         name="smooth_sketch",
-    )(radiance, up, down, left, right, corners, kernel.reshape(9, channels), test_matrix)
+    )(radiance, *border, kernel, test_matrix)
 
 
 def tree_sum(values):
@@ -295,7 +312,7 @@
     return shapes
 
 
-def wide_kernel(orders, blocks, again, b_ref, f_ref, *rest):
+def wide_kernel(orders, blocks, again, scale, b_ref, f_ref, *rest):
     o_ref, work, held, load = rest[:4]
     rest = rest[4:]
     gathered = o_ref
@@ -394,7 +411,7 @@
                 work[here] = total
                 start(reduce_copies(q, s + 1))
             else:
-                gathered[here] = total.astype(gathered.dtype)
+                gathered[here] = (total * scale).astype(gathered.dtype)
                 start(gather_copies(q, s, True))
             return
         s = 2 * steps - 1 - stage
@@ -438,7 +455,7 @@
                 copy.wait_send()
 
 
-def wide_product(basis, flattened, collective_id, again):
+def wide_product(basis, flattened, collective_id, again, scale):
     n_gy, n_gx = lax.axis_size("gy"), lax.axis_size("gx")
     pixels, cols = flattened.shape
     rows = basis.shape[1]
@@ -460,7 +477,7 @@
             scratch.append(pltpu.VMEM((2**bits - 1, *shape), jnp.float32))
     vmem = pl.BlockSpec(memory_space=pltpu.VMEM)
     return pl.pallas_call(
-        functools.partial(wide_kernel, orders, blocks, again),
+        functools.partial(wide_kernel, orders, blocks, again, scale),
         out_shape=jax.ShapeDtypeStruct((pixels, rows) if again else (rows, cols), jnp.float32),
         in_specs=[vmem, pl.BlockSpec(memory_space=pl.ANY)],
         out_specs=vmem,
@@ -541,11 +558,11 @@
     smoothed, sketch = smooth_and_sketch(radiance, kernel, test_matrix)
     flattened = smoothed.reshape(height * breadth, channels)
     first_basis = factor_basis(sketch, 0).astype(jnp.bfloat16)
-    second = wide_product(first_basis, flattened, 2, True)
+    second = wide_product(first_basis, flattened, 2, True, 1.0)
     basis_out = factor_basis(second, 1) * math.sqrt(pixel_count)
     basis_half = basis_out.astype(jnp.bfloat16)
-    projected = wide_product(basis_half, flattened, 3, False)
-    coeffs = projected * (math.sqrt(channels) / pixel_count)
+    scale = math.sqrt(channels) / pixel_count
+    coeffs = wide_product(basis_half, flattened, 3, False, scale)
     return (basis_out.reshape(height, breadth, basis_out.shape[1]), coeffs)
 
 

time: 238 us -> 229 us (0.962)
  Pallas kernels: 204 us -> 201 us
  other arithmetic: 5.27 us -> 2.46 us
  local copies, waits for them, and re-layouts: 13.8 us -> 11.2 us
    pallas_call x1, Pallas kernels: 38.4 us -> 34.7 us  [smooth_and_sketch(): pl.pallas_call(smooth_kernel, grid=(channels // block,), in_specs=[pl.Blo...]
    mul x1 -> x0, other arithmetic: 3.1 us -> none  [on_device(): coeffs = projected * (math.sqrt(channels) / pixel_count)]
where the time goes in v4:
time: 229 us
  Pallas kernels  201 us (88%)
  matrix products  13.5 us (6%)
  local copies, waits for them, and re-layouts  11.2 us (5%)
  other arithmetic  2.46 us (1%)
    pallas_call x2, Pallas kernels, wide_product(): pl.pallas_call(functools.partial(wide_kernel, orders, blocks, again, scal...  97.3 us
    pallas_call x1, Pallas kernels, smooth_and_sketch(): pl.pallas_call(smooth_kernel, grid=(channels // block,), in_specs=[pl.Blo...  34.7 us
    pallas_call x2, Pallas kernels, summed_gram(): pl.pallas_call(functools.partial(gram_kernel, n_gy, n_gx), out_shape=jax....  34.1 us
    pallas_call x2, Pallas kernels, inverse_factor(): pl.pallas_call(inverse_factor_kernel, out_shape=jax.ShapeDtypeStruct(gram...  19.9 us
    pallas_call x1, Pallas kernels, halos(): pl.pallas_call(functools.partial(halo_kernel, n_gy, n_gx), out_shape=[jax...  15 us
    dot_general x2, matrix products, factor_basis(): jnp.dot(values.T, values, precision=lax.Precision.HIGHEST, preferred_elem...  8.13 us
    dot_general x2, matrix products, factor_basis(): jnp.dot(values, inverse.T, precision=lax.Precision.HIGHEST, preferred_ele...  5.36 us
    slice x1, local copies, waits for them, and re-layouts, halos(): first, last = (radiance[:, 0], radiance[:, width - 1])  4.65 us

profile of v4, /device:TPU:0, one launch (start us, length us, event | category | flops | bytes accessed | tf_op | source)
XLA Modules:
  0.0 228.9 jit_solution(4507911090492447910)
XLA Ops:
  0.6 1.6 bitcast_convert_fusion
  2.2 4.7 %fusion = (bf16[64,1,4096]{2,1,0:T(2,128)(2,1)S(1)}, bf16[64,1,4096]{2,1,0:T(2,128)(2,1)S(1)}) fusion(bf16[64,32,4096]{2,1,0:T(8,128)(2,1)} %x_ref.3), kind=kLoop, calls=%fused_computation.9 | loop fusion | bytes 2097152 | tf_op jit(solution)/shard_map/slice | solution.py:93
  6.9 2.1 copy_bitcast_fusion
  9.0 15.0 %halo.1 = (bf16[32,4096]{1,0:T(8,128)(2,1)}, bf16[32,4096]{1,0:T(8,128)(2,1)}, bf16[64,4096]{1,0:T(8,128)(2,1)}, bf16[64,4096]{1,0:T(8,128)(2,1)}, f32[1,4096]{1...) custom-call(bf16[64,32,4096]{2,1,0:T(8,128)(2,1)} %x_ref.3, ...), custom_call_target="tpu_custom_call" | custom-call | tf_op jit(solution)/shard_map/halo/pallas_call | solution.py:102
  24.0 34.7 %smooth_sketch.1 = (bf16[64,32,4096]{2,1,0:T(8,128)(2,1)}, f32[2048,128]{1,0:T(8,128)}) custom-call(bf16[64,32,4096]{2,1,0:T(8,128)(2,1)} %x_ref.3, bf16[32,4096]{1,0:T(8,128)(2,1)} %get-tuple-element.12.up_ref, bf16[32,4096]{1,0:T(8,128)(2,1)} %get-tuple-element.13.down_ref, bf16[64,4096]{1,0:T(8,128)(2,1)} %get-tuple-element.14.left_ref, ...), custom_call_target="tpu_custom_call" | custom-call | flops 2298478592 | bytes 33554432 | tf_op jit(solution)/shard_map/smooth_sketch/pallas_call | solution.py:176
  58.8 4.0 %fusion.1.x_ref = f32[128,128]{1,0:T(8,128)} fusion(f32[2048,128]{1,0:T(8,128)} %get-tuple-element.20), kind=kOutput, calls=%fused_computation.10 | convolution fusion | flops 402653184 | bytes 1114112 | tf_op jit(solution)/shard_map/dot_general | solution.py:545
  62.7 19.9 %gram_sum.2.gram_ref = f32[128,128]{1,0:T(8,128)} custom-call(f32[128,128]{1,0:T(8,128)} %fusion.1.x_ref), custom_call_target="tpu_custom_call" | custom-call | tf_op jit(solution)/shard_map/gram_sum/pallas_call | solution.py:271
  82.6 10.0 %inverse_factor.2 = f32[128,128]{1,0:T(8,128)} custom-call(f32[128,128]{1,0:T(8,128)} %gram_sum.2.gram_ref), custom_call_target="tpu_custom_call" | custom-call | tf_op jit(solution)/shard_map/inverse_factor/pallas_call | solution.py:534
  92.6 3.1 %convolution_convert_fusion.b_ref = bf16[128,2048]{1,0:T(8,128)(2,1)} fusion(f32[128,128]{1,0:T(8,128)} %inverse_factor.2, f32[2048,128]{1,0:T(8,128)} %get-tuple-element.20), kind=kOutput, calls=%fused_computation.1 | convolution fusion | flops 402915328 | bytes 1638400 | tf_op jit(solution)/shard_map/dot_general | solution.py:549
  95.6 48.5 %wide_product.2 = f32[2048,128]{1,0:T(8,128)} custom-call(bf16[128,2048]{1,0:T(8,128)(2,1)} %convolution_convert_fusion.b_ref, bf16[2048,4096]{1,0:T(8,128)(2,1)} %bitcast.28), custom_call_target="tpu_custom_call" | custom-call | tf_op jit(solution)/shard_map/wide_product/pallas_call | solution.py:479
  144.2 4.1 %fusion.2.x_ref = f32[128,128]{1,0:T(8,128)} fusion(f32[2048,128]{1,0:T(8,128)} %wide_product.2), kind=kOutput, calls=%fused_computation.11 | convolution fusion | flops 402653184 | bytes 1114112 | tf_op jit(solution)/shard_map/dot_general | solution.py:545
  148.3 14.3 %gram_sum.3.gram_ref = f32[128,128]{1,0:T(8,128)} custom-call(f32[128,128]{1,0:T(8,128)} %fusion.2.x_ref), custom_call_target="tpu_custom_call" | custom-call | tf_op jit(solution)/shard_map/gram_sum/pallas_call | solution.py:271
  162.6 9.9 %inverse_factor.3 = f32[128,128]{1,0:T(8,128)} custom-call(f32[128,128]{1,0:T(8,128)} %gram_sum.3.gram_ref), custom_call_target="tpu_custom_call" | custom-call | tf_op jit(solution)/shard_map/inverse_factor/pallas_call | solution.py:534
  172.5 2.3 %convolution_multiply_fusion = f32[2048,128]{0,1:T(8,128)S(1)} fusion(f32[2048,128]{1,0:T(8,128)} %wide_product.2, f32[128,128]{1,0:T(8,128)} %inverse_factor.3), kind=kOutput, calls=%fused_computation | convolution fusion | flops 402915328 | bytes 2162688 | tf_op jit(solution)/shard_map/dot_general | solution.py:549
  174.8 0.9 convert_bitcast_fusion.b_ref
  175.7 48.8 %wide_product.3 = f32[128,4096]{1,0:T(8,128)} custom-call(bf16[128,2048]{1,0:T(8,128)(2,1)} %convert_bitcast_fusion.b_ref, bf16[2048,4096]{1,0:T(8,128)(2,1)} %bitcast.29), custom_call_target="tpu_custom_call" | custom-call | tf_op jit(solution)/shard_map/wide_product/pallas_call | solution.py:479
  224.5 1.3 copy.12
  225.8 3.1 %copy.19 = f32[128,4096]{1,0:T(8,128)} copy(f32[128,4096]{1,0:T(8,128)} %wide_product.3) | data formatting | bytes 4194304

commit v5 on v4

--- a/solution.py
+++ b/solution.py
@@ -441,9 +441,10 @@
         if q == 0:
             pl.semaphore_wait(barrier, len(others))
         start(reduce_copies(q, 0))
-        for p in range(q):
-            advance(p, stages[p])
-            stages[p] += 1
+        if q % 2:
+            for p in range(q - 1):
+                advance(p, stages[p])
+                stages[p] += 1
     while min(stages) < 2 * steps:
         for q in range(chunks):
             if stages[q] < 2 * steps:
@@ -459,7 +460,7 @@
     n_gy, n_gx = lax.axis_size("gy"), lax.axis_size("gx")
     pixels, cols = flattened.shape
     rows = basis.shape[1]
-    chunks = min(4, rows * cols // (16 * LANES * n_gy * n_gx))
+    chunks = min(8, rows * cols // (16 * LANES * n_gy * n_gx))
     blocks = 8
     orders = wide_orders(n_gy, n_gx, chunks)
     shapes = [kept_shapes(rows, cols // chunks, order) for order in orders]

time: 229 us -> 221 us (0.965)
  Pallas kernels: 201 us -> 192 us
    pallas_call x2, Pallas kernels: 97.3 us -> 88.6 us  [wide_product(): pl.pallas_call(functools.partial(wide_kernel, orders, blocks, again, scal...]
where the time goes in v5:
time: 221 us; the launch traced here: 220 us
  Pallas kernels  192 us (87%)
  matrix products  13.7 us (6%)
  local copies, waits for them, and re-layouts  11.2 us (5%)
  other arithmetic  2.46 us (1%)
    pallas_call x2, Pallas kernels, wide_product(): pl.pallas_call(functools.partial(wide_kernel, orders, blocks, again, scal...  88.6 us
    pallas_call x1, Pallas kernels, smooth_and_sketch(): pl.pallas_call(smooth_kernel, grid=(channels // block,), in_specs=[pl.Blo...  34.7 us
    pallas_call x2, Pallas kernels, summed_gram(): pl.pallas_call(functools.partial(gram_kernel, n_gy, n_gx), out_shape=jax....  33.9 us
    pallas_call x2, Pallas kernels, inverse_factor(): pl.pallas_call(inverse_factor_kernel, out_shape=jax.ShapeDtypeStruct(gram...  19.9 us
    pallas_call x1, Pallas kernels, halos(): pl.pallas_call(functools.partial(halo_kernel, n_gy, n_gx), out_shape=[jax...  15 us
    dot_general x2, matrix products, factor_basis(): jnp.dot(values.T, values, precision=lax.Precision.HIGHEST, preferred_elem...  8.13 us
    dot_general x2, matrix products, factor_basis(): jnp.dot(values, inverse.T, precision=lax.Precision.HIGHEST, preferred_ele...  5.62 us
    slice x1, local copies, waits for them, and re-layouts, halos(): first, last = (radiance[:, 0], radiance[:, width - 1])  4.65 us

profile of v5, /device:TPU:0, one launch (start us, length us, event | category | flops | bytes accessed | tf_op | source)
XLA Modules:
  0.0 220.2 jit_solution(1003620337551869800)
XLA Ops:
  0.6 1.6 bitcast_convert_fusion
  2.2 4.7 %fusion = (bf16[64,1,4096]{2,1,0:T(2,128)(2,1)S(1)}, bf16[64,1,4096]{2,1,0:T(2,128)(2,1)S(1)}) fusion(bf16[64,32,4096]{2,1,0:T(8,128)(2,1)} %x_ref.3), kind=kLoop, calls=%fused_computation.9 | loop fusion | bytes 2097152 | tf_op jit(solution)/shard_map/slice | solution.py:93
  6.9 2.1 copy_bitcast_fusion
  9.0 15.0 %halo.1 = (bf16[32,4096]{1,0:T(8,128)(2,1)}, bf16[32,4096]{1,0:T(8,128)(2,1)}, bf16[64,4096]{1,0:T(8,128)(2,1)}, bf16[64,4096]{1,0:T(8,128)(2,1)}, f32[1,4096]{1...) custom-call(bf16[64,32,4096]{2,1,0:T(8,128)(2,1)} %x_ref.3, ...), custom_call_target="tpu_custom_call" | custom-call | tf_op jit(solution)/shard_map/halo/pallas_call | solution.py:102
  24.0 34.7 %smooth_sketch.1 = (bf16[64,32,4096]{2,1,0:T(8,128)(2,1)}, f32[2048,128]{1,0:T(8,128)}) custom-call(bf16[64,32,4096]{2,1,0:T(8,128)(2,1)} %x_ref.3, bf16[32,4096]{1,0:T(8,128)(2,1)} %get-tuple-element.12.up_ref, bf16[32,4096]{1,0:T(8,128)(2,1)} %get-tuple-element.13.down_ref, bf16[64,4096]{1,0:T(8,128)(2,1)} %get-tuple-element.14.left_ref, ...), custom_call_target="tpu_custom_call" | custom-call | flops 2298478592 | bytes 33554432 | tf_op jit(solution)/shard_map/smooth_sketch/pallas_call | solution.py:176
  58.8 4.0 %fusion.1.x_ref = f32[128,128]{1,0:T(8,128)} fusion(f32[2048,128]{1,0:T(8,128)} %get-tuple-element.20), kind=kOutput, calls=%fused_computation.10 | convolution fusion | flops 402653184 | bytes 1114112 | tf_op jit(solution)/shard_map/dot_general | solution.py:546
  62.7 19.9 %gram_sum.2.gram_ref = f32[128,128]{1,0:T(8,128)} custom-call(f32[128,128]{1,0:T(8,128)} %fusion.1.x_ref), custom_call_target="tpu_custom_call" | custom-call | tf_op jit(solution)/shard_map/gram_sum/pallas_call | solution.py:271
  82.6 10.0 %inverse_factor.2 = f32[128,128]{1,0:T(8,128)} custom-call(f32[128,128]{1,0:T(8,128)} %gram_sum.2.gram_ref), custom_call_target="tpu_custom_call" | custom-call | tf_op jit(solution)/shard_map/inverse_factor/pallas_call | solution.py:535
  92.6 3.1 %convolution_convert_fusion.b_ref = bf16[128,2048]{1,0:T(8,128)(2,1)} fusion(f32[128,128]{1,0:T(8,128)} %inverse_factor.2, f32[2048,128]{1,0:T(8,128)} %get-tuple-element.20), kind=kOutput, calls=%fused_computation.1 | convolution fusion | flops 402915328 | bytes 1638400 | tf_op jit(solution)/shard_map/dot_general | solution.py:550
  95.6 45.4 %wide_product.2 = f32[2048,128]{1,0:T(8,128)} custom-call(bf16[128,2048]{1,0:T(8,128)(2,1)} %convolution_convert_fusion.b_ref, bf16[2048,4096]{1,0:T(8,128)(2,1)} %bitcast.28), custom_call_target="tpu_custom_call" | custom-call | tf_op jit(solution)/shard_map/wide_product/pallas_call | solution.py:480
  141.0 4.1 %fusion.2.x_ref = f32[128,128]{1,0:T(8,128)} fusion(f32[2048,128]{1,0:T(8,128)} %wide_product.2), kind=kOutput, calls=%fused_computation.11 | convolution fusion | flops 402653184 | bytes 1114112 | tf_op jit(solution)/shard_map/dot_general | solution.py:546
  145.2 14.0 %gram_sum.3.gram_ref = f32[128,128]{1,0:T(8,128)} custom-call(f32[128,128]{1,0:T(8,128)} %fusion.2.x_ref), custom_call_target="tpu_custom_call" | custom-call | tf_op jit(solution)/shard_map/gram_sum/pallas_call | solution.py:271
  159.2 9.9 %inverse_factor.3 = f32[128,128]{1,0:T(8,128)} custom-call(f32[128,128]{1,0:T(8,128)} %gram_sum.3.gram_ref), custom_call_target="tpu_custom_call" | custom-call | tf_op jit(solution)/shard_map/inverse_factor/pallas_call | solution.py:535
  169.1 2.6 %convolution_multiply_fusion = f32[2048,128]{0,1:T(8,128)S(1)} fusion(f32[2048,128]{1,0:T(8,128)} %wide_product.2, f32[128,128]{1,0:T(8,128)} %inverse_factor.3), kind=kOutput, calls=%fused_computation | convolution fusion | flops 402915328 | bytes 2162688 | tf_op jit(solution)/shard_map/dot_general | solution.py:550
  171.7 0.9 convert_bitcast_fusion.b_ref
  172.5 43.2 %wide_product.3 = f32[128,4096]{1,0:T(8,128)} custom-call(bf16[128,2048]{1,0:T(8,128)(2,1)} %convert_bitcast_fusion.b_ref, bf16[2048,4096]{1,0:T(8,128)(2,1)} %bitcast.29), custom_call_target="tpu_custom_call" | custom-call | tf_op jit(solution)/shard_map/wide_product/pallas_call | solution.py:480
  215.8 1.3 copy.12
  217.1 3.1 %copy.19 = f32[128,4096]{1,0:T(8,128)} copy(f32[128,4096]{1,0:T(8,128)} %wide_product.3) | data formatting | bytes 4194304
